TPU v7x, 512 devices: a whole 4x4x16 slice. The times are simulated.
512 devices in a mesh: feat: 32 (over y, z_hi, core), layer: 4 (over x), dp: 4 (over z_lo).
Axes of the slice: x: 4, y: 4, z: 16 (z_hi: 4, z_lo: 4; z = z_hi * 4 + z_lo), core: 2. Of those that a mesh axis runs over, the one named last changes fastest.
Arguments:
- residual: bfloat16 [4, 1024, 2304], P('layer', 'dp'), may hold values from -6 to 6
- enc_weight: bfloat16 [4, 2304, 8192], P('layer', None, 'feat'), may hold values from -0.125 to 0.125
- enc_bias: float32 [4, 8192], P('layer', 'feat'), may hold values from -0.6 to 0.3
- dec_weight: bfloat16 [4, 4, 8192, 2304], P(None, 'layer', 'feat', 'dp'), may hold values from -0.046875 to 0.046875
- dec_bias: float32 [4, 2304], P('layer', 'dp'), may hold values from -3 to 3
- target: bfloat16 [4, 1024, 2304], P('layer', 'feat', 'dp'), may hold values from -6 to 6
Outputs:
- enc_grad: bfloat16 [4, 2304, 8192], P('layer', 'dp', 'feat')
- dec_grad: bfloat16 [4, 4, 8192, 2304], P(None, 'layer', 'feat', 'dp')
All inputs are finite; a program needn't handle non-finite values.
Results may differ from a plain program's by a relative error of at most 0.023.
Values may be sent and summed in bfloat16 or wider, within the bound.
A program may use at most 64 MiB of HBM per device.

v0:
```python
import math

import jax
import jax.numpy as jnp
from jax import lax
from jax.sharding import PartitionSpec as P


def laid_out(parts, dim):
    shape = list(parts.shape[1:])
    shape[dim] *= parts.shape[0]
    return jnp.moveaxis(parts, 0, dim).reshape(shape)


def copy_for_each(value, axis):
    copies = jnp.broadcast_to(value, (lax.axis_size(axis), *value.shape))
    return lax.all_to_all(copies, axis, split_axis=0, concat_axis=0, tiled=True)


def collect(value, axis, dim):
    return laid_out(copy_for_each(value, axis), dim)


def split_up(value, dim, count):
    shape = value.shape
    parts = value.reshape(*shape[:dim], count, shape[dim] // count, *shape[dim + 1 :])
    return jnp.moveaxis(parts, dim, 0)


def summed_on_arrival(value, axis, dim):
    count = lax.axis_size(axis)
    parts = lax.all_to_all(split_up(value, dim, count), axis, 0, 0, tiled=True)
    return jnp.sum(parts.astype(jnp.float32), axis=0)


def shards(residual, enc_weight, enc_bias, dec_weight, dec_bias, target):
    resid_rows = residual[0]
    pre_act = jnp.dot(resid_rows, enc_weight[0], preferred_element_type=jnp.float32) + enc_bias
    positive = jnp.maximum(pre_act, 0.0)
    codes_own = (positive * positive).astype(jnp.bfloat16)
    layer_count = dec_weight.shape[0]
    feat_local = codes_own.shape[1]
    gathered = collect(codes_own, ("layer", "dp"), 0)
    codes_all = gathered.reshape(layer_count, -1, feat_local)
    token_count = codes_all.shape[1]
    causal = jnp.arange(layer_count) <= lax.axis_index("layer")
    codes_all = jnp.where(causal[:, None, None], codes_all, jnp.zeros_like(codes_all))
    weights = dec_weight[:, 0]
    loss_scale = 1.0 / math.sqrt(token_count)
    recon = lax.psum_scatter(
        jnp.einsum("lnf,lfd->nd", codes_all, weights, preferred_element_type=jnp.float32).astype(
            jnp.bfloat16
        ),
        "feat",
        scatter_dimension=0,
        tiled=True,
    ).astype(jnp.float32)
    error_rows = recon + dec_bias - target[0].astype(jnp.float32)
    grad_rows = (error_rows * loss_scale).astype(jnp.bfloat16)
    grad_all = lax.all_gather(grad_rows, "feat", axis=0, tiled=True)
    dec_local = jnp.einsum("lnf,nd->lfd", codes_all, grad_all, preferred_element_type=jnp.float32)
    dec_out = dec_local.astype(jnp.bfloat16)[:, None]
    back_terms = jnp.einsum("nd,lfd->lnf", grad_all, weights, preferred_element_type=jnp.float32)
    back_terms = jnp.where(causal[:, None, None], back_terms, jnp.zeros_like(back_terms))
    back_sum = summed_on_arrival(
        back_terms.reshape(-1, feat_local).astype(jnp.bfloat16), ("layer", "dp"), 0
    )
    code_grad = (back_sum * 2.0 * positive).astype(jnp.bfloat16)
    enc_sum = summed_on_arrival(
        jnp.einsum("nd,nf->df", resid_rows, code_grad, preferred_element_type=jnp.float32).astype(
            jnp.bfloat16
        ),
        "dp",
        0,
    )
    return (enc_sum.astype(jnp.bfloat16)[None], dec_out)


def solution(mesh):
    in_specs = (
        P("layer", "dp", None),
        P("layer", None, "feat"),
        P("layer", "feat"),
        P(None, "layer", "feat", "dp"),
        P("layer", "dp"),
        P("layer", "feat", "dp"),
    )
    out_specs = (P("layer", "dp", "feat"), P(None, "layer", "feat", "dp"))
    return jax.shard_map(shards, mesh=mesh, in_specs=in_specs, out_specs=out_specs, check_vma=False)
```

profile of v0, /device:TPU:6, one launch (start us, length us, event | category | flops | bytes accessed | tf_op | source)
XLA Modules:
  0.0 361.0 jit_solution(3328442778969062029)
XLA Ops:
  7.2 0.0 copy-start
  7.2 2.2 multiply_convert_fusion.1
  9.4 1.5 broadcast_in_dim.35
  10.9 9.4 %all-to-all-start = ((bf16[16,256,256]{2,1,0:T(8,128)(2,1)}), bf16[16,256,256]{2,1,0:T(8,128)(2,1)S(1)}, u32[]{:S(2)}, u32[]{:S(2)}) async-start(bf16[16,256,256]{2,1,0:T(8,128)(2,1)} %broadcast_in_dim.35), calls=%async_computation | async-start | bytes 4194304 | tf_op jit(solution)/shard_map/all_to_all | solution.py:17
  20.4 0.0 reduce-scatter.2.cloned.1.call-start
  20.4 47.3 %all-to-all-done = bf16[16,256,256]{2,1,0:T(8,128)(2,1)S(1)} async-done(((bf16[16,256,256]{2,1,0:T(8,128)(2,1)}), bf16[16,256,256]{2,1,0:T(8,128)(2,1)S(1)}, u32[]{:S(2)}, u32[]{:S(2)}) %all-to-all-start) | async-done | bytes 2097184 | tf_op jit(solution)/shard_map/all_to_all | solution.py:17
  67.7 0.2 bitcast_select_fusion
  68.0 0.0 copy-start.2
  68.0 1.3 copy-done.2
  69.3 0.0 copy-done
  69.3 2.9 bitcast_convert_fusion
  72.2 0.0 copy-start.4
  72.2 0.0 copy-start.3
  72.2 0.0 reduce-scatter.2.cloned.1.call-update
  72.2 0.0 all-gather.2.cloned.1.call-start
  72.3 0.6 copy-done.4
  72.9 116.9 %reduce-scatter.2.cloned.1.call-done = bf16[32,576]{1,0:T(8,128)(2,1)} async-done(((bf16[1024,576]{1,0:T(8,128)(2,1)}), bf16[32,576]{1,0:T(8,128)(2,1)}) %reduce-scatter.2.cloned.1.call-update) | async-done | bytes 36880 | tf_op jit(solution)/shard_map/reduce_scatter | solution.py:50
  189.8 0.0 copy-done.3
  189.8 1.4 fusion.22
  191.2 0.0 all-gather.2.cloned.1.call-update
  191.2 70.0 %all-gather.2.cloned.1.call-done = bf16[1024,576]{1,0:T(8,128)(2,1)} async-done(((bf16[32,576]{1,0:T(8,128)(2,1)}), bf16[1024,576]{1,0:T(8,128)(2,1)}) %all-gather.2.cloned.1.call-update) | async-done | bytes 1179664 | tf_op jit(solution)/shard_map/all_gather | solution.py:60
  261.3 3.1 select_convert_fusion
  264.4 54.3 %all_to_all.15 = bf16[16,256,256]{2,1,0:T(8,128)(2,1)S(1)} all-to-all(bf16[16,256,256]{2,1,0:T(8,128)(2,1)S(1)} %bitcast.53), channel_id=1, replica_groups=mesh['feat'=32,'layer'=4,'dp'=4] {'layer','dp'}, dimensions={0} | all-to-all | bytes 4194304 | tf_op jit(solution)/shard_map/all_to_all | solution.py:32
  318.7 0.0 copy-start.1
  318.7 0.3 convert_reduce_fusion
  319.0 1.0 copy-done.1
  319.9 0.5 fusion
  320.5 1.4 copy.9
  321.9 3.5 all-to-all-start.2
  325.4 4.4 %fusion.1 = bf16[4,1,256,576]{2,3,1,0:T(8,128)(2,1)} fusion(bf16[4,1024,256]{2,1,0:T(8,128)(2,1)} %copy-done.2, bf16[1024,576]{1,0:T(8,128)(2,1)} %all-gather.2.cloned.1.call-done), kind=kOutput, calls=%fused_computation.7 | convolution fusion | flops 1208549376 | bytes 4456448 | tf_op jit(solution)/shard_map/lnf,nd->lfd/dot_general | solution.py:61
  329.8 23.4 %all-to-all-done.2 = bf16[4,576,256]{2,1,0:T(8,128)(2,1)S(1)} async-done(((bf16[4,576,256]{2,1,0:T(8,128)(2,1)}), bf16[4,576,256]{2,1,0:T(8,128)(2,1)S(1)}, u32[]{:S(2)}, u32[]{:S(2)}) %all-to-all-start.2) | async-done | bytes 1179680 | tf_op jit(solution)/shard_map/all_to_all | solution.py:32
  353.2 0.9 reduce_sum.22
  (2 shorter events, 0.0 us)
Async XLA Ops:
  7.2 62.1 %copy-start = (bf16[4,1,256,576]{2,3,1,0:T(8,128)(2,1)S(1)}, bf16[4,1,256,576]{2,3,1,0:T(8,128)(2,1)}, u32[]{:S(2)}) copy-start(bf16[4,1,256,576]{2,3,1,0:T(8,128)(2,1)} %param.9) | copy-start | bytes 3538948
  10.9 56.8 %all-to-all-start = ((bf16[16,256,256]{2,1,0:T(8,128)(2,1)}), bf16[16,256,256]{2,1,0:T(8,128)(2,1)S(1)}, u32[]{:S(2)}, u32[]{:S(2)}) async-start(bf16[16,256,256]{2,1,0:T(8,128)(2,1)} %broadcast_in_dim.35), calls=%async_computation | async-start | bytes 4194304 | tf_op jit(solution)/shard_map/all_to_all | solution.py:17
  20.4 169.5 %reduce-scatter.2.cloned.1.call-start = ((), (), s32[]{:S(2)}) async-start(), calls=%async_computation.4 | async-start | bytes 1351680 | tf_op jit(solution)/shard_map/reduce_scatter | solution.py:50
  68.0 1.3 copy-start.2
  72.2 0.7 copy-start.4
  72.2 117.6 %copy-start.3 = (bf16[1,32,576]{2,1,0:T(8,128)(2,1)S(1)}, bf16[1,32,576]{2,1,0:T(8,128)(2,1)}, u32[]{:S(2)}) copy-start(bf16[1,32,576]{2,1,0:T(8,128)(2,1)} %param.11) | copy-start | bytes 110596
  72.2 189.1 %all-gather.2.cloned.1.call-start = ((), (), s32[]{:S(2)}) async-start(), calls=%async_computation.5 | async-start | bytes 1351680 | tf_op jit(solution)/shard_map/all_gather | solution.py:60
  318.7 1.3 copy-start.1
  321.9 31.4 %all-to-all-start.2 = ((bf16[4,576,256]{2,1,0:T(8,128)(2,1)}), bf16[4,576,256]{2,1,0:T(8,128)(2,1)S(1)}, u32[]{:S(2)}, u32[]{:S(2)}) async-start(bf16[4,576,256]{2,1,0:T(8,128)(2,1)} %bitcast.11), calls=%async_computation.3 | async-start | bytes 2359296 | tf_op jit(solution)/shard_map/all_to_all | solution.py:32
Sparse Core Ops, SparseCore 0:
  72.3 117.4 reduce-scatter.1
  194.0 67.2 all-gather.1
where the time goes:
time: 364 us; the launch traced here: 361 us
  waiting for transfers between devices  258 us (71%)
  blocking collectives  54.3 us (15%)
  between operations  14.1 us (4%)
  matrix products  13.1 us (4%)
  starting transfers between devices  13 us (4%)
  local copies, waits for them, and re-layouts  5.86 us (2%)
    reduce_scatter x1, waiting for transfers between devices, shards(): lax.psum_scatter(jnp.einsum('lnf,lfd->nd', codes_all, weights, preferred_...  117 us
    all_gather x1, waiting for transfers between devices, shards(): grad_all = lax.all_gather(grad_rows, 'feat', axis=0, tiled=True)  70 us
    all_to_all x1, blocking collectives, summed_on_arrival(): parts = lax.all_to_all(split_up(value, dim, count), axis, 0, 0, tiled=True)  54.3 us
    all_to_all x1, waiting for transfers between devices, copy_for_each(): return lax.all_to_all(copies, axis, split_axis=0, concat_axis=0, tiled=True)  47.3 us
    all_to_all x1, waiting for transfers between devices, summed_on_arrival(): parts = lax.all_to_all(split_up(value, dim, count), axis, 0, 0, tiled=True)  23.4 us
    all_to_all x1, starting transfers between devices, copy_for_each(): return lax.all_to_all(copies, axis, split_axis=0, concat_axis=0, tiled=True)  9.43 us
  transfers between devices with their start and end apart: 4, of which 4 were waited for; matrix products, arithmetic and copies ran while one was open for 1% of the time, Pallas kernels for 0%

commit v1 on v0

v1 whole, which is shorter than its diff:
```python
import math

import jax
import jax.numpy as jnp
from jax import lax
from jax.experimental import pallas as pl
from jax.experimental.pallas import tpu as pltpu
from jax.sharding import PartitionSpec as P

MESH = pl.DeviceIdType.MESH
BF = jnp.bfloat16
F32 = jnp.float32
WIN = 640

SEMS = dict(
    load=3, ar=16, a_right=4, a_left=4, a_n1=4, a_n2=4, a_rl=4,
    rr=4, rr_s=4, rc=3, rc_s=3,
    pc=4, pc_s=4,
    yb=24, yb_s=24, zb=6, zb_s=6,
    cz=4, cz_s=4, cy=16, cy_s=16, cc=16, cc_s=16,
    xr=4, xl=4, xe=4, x_s=12, zc=8, zc_s=4, e=4, e_right=4, e_left=4,
)

SCRATCH = dict(
    resid=((256, 2304), BF), w=((2304, 256), BF), wt=((4, 576, 256), BF),
    pos=((256, 256), F32), codes=((16, 256, 256), BF),
    rw=((4, 256, WIN), BF), rwt=((4, WIN, 256), BF),
    acc=((4, 4, 2, 32, 576), F32), po=((4, 4, 32, 576), BF), pc=((4, 4, 32, 576), BF),
    yst=((24, 16, 576), BF), yb=((24, 16, 576), BF),
    tz=((4, 32, 576), F32), zst=((6, 16, 576), BF), zb=((6, 16, 576), BF),
    g=((4, 4, 2, 32, 576), BF), gt=((4, 576, 256), BF),
    bt=((16, 256, 256), BF), xr=((4, 256, 256), BF), xl=((4, 256, 256), BF), xe=((4, 256, 256), BF),
    s=((4, 256, 256), F32), ss=((4, 256, 256), BF), zc=((8, 256, 256), BF),
    cg=((4, 256, 256), BF), eacc=((WIN, 256), F32),
)


def body(*refs):
    resid_h, w_h, bias, wt_h, dbias, target, enc_o, dec_o = refs[:8]
    R = dict(zip(SCRATCH, refs[8 : 8 + len(SCRATCH)]))
    S = dict(zip(SEMS, refs[8 + len(SCRATCH) :]))
    resid, w, wt, pos, codes = R["resid"], R["w"], R["wt"], R["pos"], R["codes"]
    f = lax.axis_index("feat")
    t = lax.axis_index("layer")
    d = lax.axis_index("dp")
    c, z, y = lax.rem(f, 2), lax.rem(f // 2, 4), f // 8

    def at(yy, zz, core):
        return (lax.rem(yy + 8, 4) * 4 + lax.rem(zz + 8, 4)) * 2 + core

    def along_z(k):
        g = lax.rem(z * 4 + d + k + 16, 16)
        return (at(y, g // 4, c), t, lax.rem(g, 4))

    dev_core = (at(y, z, 1 - c), t, d)
    dev_yp, dev_ym = (at(y + 1, z, c), t, d), (at(y - 1, z, c), t, d)
    dev_zp, dev_zm = (at(y, z + 1, c), t, d), (at(y, z - 1, c), t, d)
    dev_xp, dev_xm = (f, lax.rem(t + 1, 4), d), (f, lax.rem(t + 3, 4), d)
    dev_r, dev_l = (f, t, lax.rem(d + 1, 4)), (f, t, lax.rem(d + 3, 4))

    def copy(src, dst, ssem, rsem, dev):
        return pltpu.make_async_remote_copy(
            src_ref=src, dst_ref=dst, send_sem=ssem, recv_sem=rsem, device_id=dev, device_id_type=MESH
        )

    def arrived(dst, rsem):
        copy(dst, dst, S["load"].at[0], rsem, dev_core).wait_recv()

    def sent(src, ssem):
        copy(src, src, ssem, S["load"].at[0], dev_core).wait_send()

    loads = [
        pltpu.make_async_copy(resid_h.at[0], resid, S["load"].at[0]),
        pltpu.make_async_copy(w_h.at[0], w, S["load"].at[1]),
        pltpu.make_async_copy(wt_h, wt, S["load"].at[2]),
    ]
    for one in loads:
        one.start()

    barrier = pltpu.get_barrier_semaphore()
    partners = [dev_core, dev_yp, dev_ym, dev_zp, dev_zm, dev_xp, dev_xm]
    partners += [along_z(k) for k in (1, -1, 2, -2)]
    for dev in partners:
        pl.semaphore_signal(barrier, inc=1, device_id=dev, device_id_type=MESH)
    pl.semaphore_wait(barrier, len(partners))

    loads[0].wait()
    loads[1].wait()
    pre = jnp.dot(resid[...], w[...], preferred_element_type=F32) + bias[...]
    positive = jnp.maximum(pre, 0.0)
    pos[...] = positive
    codes[t * 4 + d] = (positive * positive).astype(BF)

    def offset(i):
        half = (i + 1) // 2
        return jnp.where(lax.rem(i, 2) == 1, -half, half)

    def relays(b):
        return ((t == 0) & (b < 2)) | ((t == 2) & (b >= 2)) | (t == 3)

    relay_from = jnp.where(t == 3, 0, 1)
    dev_relay = (f, jnp.where(t == 3, 2, 3), d)

    def second(b):
        return (t == 0) | ((t == 1) & (b < 2))

    @pl.loop(0, 10)
    def _(i):
        b = d + offset(i)

        @pl.when((i < 7) & (b >= 0) & (b < 4))
        def _():
            blk = codes.at[t * 4 + b]
            sem = S["ar"].at[t * 4 + b]

            @pl.when(i > 0)
            def _():
                arrived(blk, sem)

            @pl.when((b <= d) & (d < 3))
            def _():
                copy(blk, blk, S["a_right"].at[b], sem, dev_r).start()

            @pl.when((b >= d) & (d > 0))
            def _():
                copy(blk, blk, S["a_left"].at[b], sem, dev_l).start()

            @pl.when(t < 3)
            def _():
                copy(blk, blk, S["a_n1"].at[b], sem, dev_xp).start()

            @pl.when(second(b))
            def _():
                copy(blk, blk, S["a_n2"].at[b], sem, dev_xm).start()

        rb = d + offset(jnp.maximum(i - 3, 0))

        @pl.when((i >= 3) & (rb >= 0) & (rb < 4))
        def _():
            @pl.when(relays(rb))
            def _():
                blk = codes.at[relay_from * 4 + rb]
                sem = S["ar"].at[relay_from * 4 + rb]
                arrived(blk, sem)
                copy(blk, blk, S["a_rl"].at[rb], sem, dev_relay).start()

    def start_col(k):
        return pl.multiple_of(k * 576 - 64 * lax.rem(k, 2), 128)

    rw = R["rw"]

    def move_cols(k, lo, size, slot):
        rows = pl.ds(pl.multiple_of(c * 128 + lo, 64), size)
        dev = along_z(k)
        src = resid.at[rows, pl.ds(start_col(dev[2]), WIN)]
        return copy(src, rw.at[d, rows], S["rr_s"].at[slot], S["rr"].at[slot], dev)

    col_moves = [move_cols(1, 0, 128, 0), move_cols(-1, 0, 128, 1), move_cols(2, 0, 64, 2), move_cols(-2, 64, 64, 3)]
    for one in col_moves:
        one.start()
    rw[d] = resid[:, pl.ds(start_col(d), WIN)]

    @pl.loop(0, 12)
    def _(i):
        l, b = i // 4, lax.rem(i, 4)
        relayed = relays(b) & (l == relay_from)

        @pl.when((l < t) & jnp.logical_not(relayed))
        def _():
            arrived(codes.at[i], S["ar"].at[i])

    loads[2].wait()

    acc, po, pc = R["acc"], R["po"], R["pc"]

    @pl.loop(0, 4)
    def _(b):
        for top in range(4):
            @pl.when(t == top)
            def _():
                total = None
                for l in range(top + 1):
                    term = lax.dot_general(
                        codes[l * 4 + b], wt[l], (((1,), (1,)), ((), ())), preferred_element_type=F32
                    )
                    total = term if total is None else total + term
                acc[b] = total.reshape(4, 2, 32, 576)

        po[b] = acc[b, :, 1 - c].astype(BF)
        copy(po.at[b], pc.at[b], S["pc_s"].at[b], S["pc"].at[b], dev_core).start()

    half = pl.ds(pl.multiple_of(c * 128, 128), 128)
    slots = [lax.rem(d + 3, 4), lax.rem(d + 1, 4), lax.rem(d + 2, 4)]
    first_half = pl.ds(pl.multiple_of(c * 128, 64), 64)
    last_half = pl.ds(pl.multiple_of(c * 128 + 64, 64), 64)
    arrived(rw.at[slots[0], half], S["rr"].at[0])
    arrived(rw.at[slots[1], half], S["rr"].at[1])
    arrived(rw.at[slots[2], first_half], S["rr"].at[2])
    arrived(rw.at[slots[2], last_half], S["rr"].at[3])
    core_moves = [
        copy(rw.at[k, half], rw.at[k, half], S["rc_s"].at[n], S["rc"].at[n], dev_core) for n, k in enumerate(slots)
    ]
    for one in core_moves:
        one.start()

    @pl.loop(0, 4)
    def _(b):
        arrived(pc.at[b], S["pc"].at[b])

    yst, yb = R["yst"], R["yb"]

    def chunk_z(i):
        return lax.rem(z + jnp.where(i == 0, 2, jnp.where(i == 1, 1, jnp.where(i == 2, 3, 0))), 4)

    def partial(yy, zz, h):
        rows = pl.ds(16 * h, 16)
        yy = lax.rem(yy + 4, 4)
        return acc[yy, zz, c, rows] + pc[yy, zz, rows].astype(F32)

    def y_send(i, k, value, dev):
        n = i * 6 + k
        yst[n] = value.astype(BF)
        copy(yst.at[n], yb.at[n], S["yb_s"].at[n], S["yb"].at[n], dev).start()

    def y_take(i, k):
        n = i * 6 + k
        arrived(yb.at[n], S["yb"].at[n])
        return yb[n].astype(F32)

    @pl.loop(0, 4)
    def _(i):
        zz = chunk_z(i)
        y_send(i, 0, partial(y + 2, zz, 0), dev_yp)
        y_send(i, 1, partial(y + 2, zz, 1), dev_ym)
        y_send(i, 2, partial(y + 1, zz, 1), dev_yp)
        y_send(i, 3, partial(y - 1, zz, 0), dev_ym)

    @pl.loop(0, 4)
    def _(i):
        zz = chunk_z(i)
        y_send(i, 4, partial(y + 1, zz, 0) + y_take(i, 0), dev_yp)
        y_send(i, 5, partial(y - 1, zz, 1) + y_take(i, 1), dev_ym)

    tz, zst, zb = R["tz"], R["zst"], R["zb"]

    def z_send(k, value, dev):
        zst[k] = value.astype(BF)
        copy(zst.at[k], zb.at[k], S["zb_s"].at[k], S["zb"].at[k], dev).start()

    def z_take(k):
        arrived(zb.at[k], S["zb"].at[k])
        return zb[k].astype(F32)

    @pl.loop(0, 4)
    def _(i):
        zz = chunk_z(i)
        top_half = partial(y, zz, 0) + y_take(i, 3) + y_take(i, 4)
        low_half = partial(y, zz, 1) + y_take(i, 2) + y_take(i, 5)
        tz[i, pl.ds(0, 16)] = top_half
        tz[i, pl.ds(16, 16)] = low_half

        @pl.when(i == 0)
        def _():
            z_send(0, top_half, dev_zp)
            z_send(1, low_half, dev_zm)

        @pl.when(i == 1)
        def _():
            z_send(2, low_half, dev_zp)

        @pl.when(i == 2)
        def _():
            z_send(3, top_half, dev_zm)

    z_send(4, tz[1, pl.ds(0, 16)] + z_take(0), dev_zp)
    z_send(5, tz[2, pl.ds(16, 16)] + z_take(1), dev_zm)
    scale = 1.0 / math.sqrt(1024)
    g = R["g"]
    for h, ks in enumerate(((3, 4), (2, 5))):
        rows = pl.ds(16 * h, 16)
        recon = tz[3, rows] + z_take(ks[0]) + z_take(ks[1])
        err = recon + dbias[...] - target[0, rows].astype(F32)
        g[y, z, c, rows] = (err * scale).astype(BF)

    up, down = pl.ds(0, 16), pl.ds(16, 16)

    def block_z(j):
        return lax.rem(z + jnp.where(j == 0, 0, jnp.where(j == 1, 3, jnp.where(j == 2, 1, 2))), 4)

    def to_core(yy, zz):
        n = yy * 4 + zz
        blk = g.at[yy, zz, c]
        copy(blk, blk, S["cc_s"].at[n], S["cc"].at[n], dev_core).start()

    def to_y(j):
        blk = g.at[y, block_z(j), c]
        copy(blk, blk, S["cy_s"].at[j * 4], S["cy"].at[j * 4], dev_yp).start()
        copy(blk, blk, S["cy_s"].at[j * 4 + 1], S["cy"].at[j * 4 + 1], dev_ym).start()
        to_core(y, block_z(j))

    ym, yp, y2 = lax.rem(y + 3, 4), lax.rem(y + 1, 4), lax.rem(y + 2, 4)
    zm, zp, z2 = lax.rem(z + 3, 4), lax.rem(z + 1, 4), lax.rem(z + 2, 4)

    own = g.at[y, z, c]
    copy(own, own, S["cz_s"].at[0], S["cz"].at[0], dev_zp).start()
    copy(own, own, S["cz_s"].at[1], S["cz"].at[1], dev_zm).start()
    to_y(0)
    arrived(g.at[y, zm, c], S["cz"].at[0])
    part = g.at[y, zm, c, up]
    copy(part, part, S["cz_s"].at[2], S["cz"].at[2], dev_zp).start()
    to_y(1)
    arrived(g.at[y, zp, c], S["cz"].at[1])
    part = g.at[y, zp, c, down]
    copy(part, part, S["cz_s"].at[3], S["cz"].at[3], dev_zm).start()
    to_y(2)

    def y_forward(j):
        zz = block_z(j)
        arrived(g.at[ym, zz, c], S["cy"].at[j * 4])
        part = g.at[ym, zz, c, up]
        copy(part, part, S["cy_s"].at[j * 4 + 2], S["cy"].at[j * 4 + 2], dev_yp).start()
        to_core(ym, zz)
        arrived(g.at[yp, zz, c], S["cy"].at[j * 4 + 1])
        part = g.at[yp, zz, c, down]
        copy(part, part, S["cy_s"].at[j * 4 + 3], S["cy"].at[j * 4 + 3], dev_ym).start()
        to_core(yp, zz)

    y_forward(0)
    arrived(g.at[y, z2, c, up], S["cz"].at[2])
    arrived(g.at[y, z2, c, down], S["cz"].at[3])
    to_y(3)

    @pl.loop(1, 4)
    def _(j):
        y_forward(j)

    @pl.loop(0, 4)
    def _(j):
        zz = block_z(j)
        arrived(g.at[y2, zz, c, up], S["cy"].at[j * 4 + 2])
        arrived(g.at[y2, zz, c, down], S["cy"].at[j * 4 + 3])
        to_core(y2, zz)

    @pl.loop(0, 16)
    def _(n):
        arrived(g.at[n // 4, lax.rem(n, 4), 1 - c], S["cc"].at[n])

    bt, xr, xl, xe, s, ss, zc = R["bt"], R["xr"], R["xl"], R["xe"], R["s"], R["ss"], R["zc"]
    gt = R["gt"]

    def order(i):
        return jnp.where(i == 0, 0, jnp.where(i == 1, 3, i - 1))

    def x_send(k, b, l, dst, name, dev):
        copy(bt.at[l * 4 + b], dst.at[b], S["x_s"].at[k * 4 + b], S[name].at[b], dev).start()

    @pl.loop(0, 4)
    def _(i):
        b = order(i)
        for l in (1, 2, 0, 3):
            @pl.when(t >= l)
            def _():
                bt[l * 4 + b] = jnp.dot(
                    g[b].reshape(256, 576), wt[l], preferred_element_type=F32
                ).astype(BF)

        @pl.when(t == 1)
        def _():
            x_send(0, b, 0, xr, "xr", dev_xm)

        @pl.when(t == 2)
        def _():
            x_send(0, b, 0, xl, "xl", dev_xp)

            @pl.when(b < 2)
            def _():
                x_send(1, b, 1, xr, "xr", dev_xm)

        @pl.when(t == 3)
        def _():
            @pl.when(b < 2)
            def _():
                x_send(1, b, 1, xe, "xe", dev_xp)

            @pl.when(b >= 2)
            def _():
                x_send(1, b, 1, xe, "xe", dev_xm)

            x_send(2, b, 2, xr, "xr", dev_xm)

    @pl.loop(0, 4)
    def _(b):
        gt[b] = g[b].reshape(256, 576).T

    def add_in(l, b, other, name):
        arrived(other.at[b], S[name].at[b])
        bt[l * 4 + b] = (bt[l * 4 + b].astype(F32) + other[b].astype(F32)).astype(BF)

    @pl.loop(0, 5)
    def _(i):
        b = order(i)

        @pl.when(i < 4)
        def _():
            @pl.when(t == 3)
            def _():
                add_in(0, b, xl, "xl")
                x_send(0, b, 0, xl, "xl", dev_xp)

            @pl.when((t == 2) & (b >= 2))
            def _():
                add_in(1, b, xe, "xe")
                x_send(1, b, 1, xr, "xr", dev_xm)

            @pl.when((t == 0) & (b < 2))
            def _():
                arrived(xe.at[b], S["xe"].at[b])
                copy(xe.at[b], xl.at[b], S["x_s"].at[b], S["xl"].at[b], dev_xp).start()

            @pl.when(i <= t)
            def _():
                total = None
                for k in range(4):
                    term = jnp.dot(gt[k], codes[i * 4 + k], preferred_element_type=F32)
                    total = term if total is None else total + term
                dec_o[i] = total.astype(BF)

            @pl.when(i > t)
            def _():
                dec_o[i] = jnp.zeros((576, 256), BF)

        @pl.when(i > 0)
        def _():
            q = order(jnp.maximum(i - 1, 0))
            s[q] = bt[t * 4 + q].astype(F32)

            @pl.when(t < 3)
            def _():
                arrived(xr.at[q], S["xr"].at[q])
                s[q] += xr[q].astype(F32)

            @pl.when((t == 0) | ((t == 1) & (q < 2)))
            def _():
                arrived(xl.at[q], S["xl"].at[q])
                s[q] += xl[q].astype(F32)

            @pl.when((d < q) & (d > 0))
            def _():
                arrived(zc.at[q], S["zc"].at[q])
                s[q] += zc[q].astype(F32)

            @pl.when((d > q) & (d < 3))
            def _():
                arrived(zc.at[4 + q], S["zc"].at[4 + q])
                s[q] += zc[4 + q].astype(F32)

            @pl.when(d < q)
            def _():
                ss[q] = s[q].astype(BF)
                copy(ss.at[q], zc.at[q], S["zc_s"].at[q], S["zc"].at[q], dev_r).start()

            @pl.when(d > q)
            def _():
                ss[q] = s[q].astype(BF)
                copy(ss.at[q], zc.at[4 + q], S["zc_s"].at[q], S["zc"].at[4 + q], dev_l).start()

    rwt = R["rwt"]
    for n, k in enumerate(slots):
        other_half = pl.ds(pl.multiple_of((1 - c) * 128, 128), 128)
        arrived(rw.at[k, other_half], S["rc"].at[n])

    @pl.loop(0, 4)
    def _(k):
        rwt[k] = rw[k].T

    @pl.when(d > 0)
    def _():
        arrived(zc.at[d], S["zc"].at[d])
        s[d] += zc[d].astype(F32)

    @pl.when(d < 3)
    def _():
        arrived(zc.at[4 + d], S["zc"].at[4 + d])
        s[d] += zc[4 + d].astype(F32)

    cg, eacc = R["cg"], R["eacc"]
    cg[d] = (s[d] * 2.0 * pos[...]).astype(BF)

    eacc[...] = jnp.zeros_like(eacc)

    @pl.loop(0, 7)
    def _(i):
        b = d + offset(i)

        @pl.when((b >= 0) & (b < 4))
        def _():
            blk, sem = cg.at[b], S["e"].at[b]

            @pl.when(i > 0)
            def _():
                arrived(blk, sem)

            @pl.when((b <= d) & (d < 3))
            def _():
                copy(blk, blk, S["e_right"].at[b], sem, dev_r).start()

            @pl.when((b >= d) & (d > 0))
            def _():
                copy(blk, blk, S["e_left"].at[b], sem, dev_l).start()

            eacc[...] += jnp.dot(rwt[b], cg[b], preferred_element_type=F32)

    shift = pl.multiple_of(64 * lax.rem(d, 2), 64)
    enc_o[0] = eacc[pl.ds(shift, 576)].astype(BF)

    @pl.loop(0, 4)
    def _(b):
        blk = codes.at[b]

        @pl.when((b <= d) & (d < 3))
        def _():
            sent(blk, S["a_right"].at[b])
            sent(blk, S["e_right"].at[b])

        @pl.when((b >= d) & (d > 0))
        def _():
            sent(blk, S["a_left"].at[b])
            sent(blk, S["e_left"].at[b])

        @pl.when(t < 3)
        def _():
            sent(blk, S["a_n1"].at[b])

        @pl.when(second(b))
        def _():
            sent(blk, S["a_n2"].at[b])

        @pl.when(relays(b))
        def _():
            sent(blk, S["a_rl"].at[b])

        sent(po.at[b], S["pc_s"].at[b])

        @pl.when((t > 0) | (b < 2))
        def _():
            sent(blk, S["x_s"].at[b])

        @pl.when(t >= 2)
        def _():
            sent(blk, S["x_s"].at[4 + b])

        @pl.when(t == 3)
        def _():
            sent(blk, S["x_s"].at[8 + b])

        @pl.when(d != b)
        def _():
            sent(blk, S["zc_s"].at[b])

        sent(own, S["cy_s"].at[b * 4])
        sent(own, S["cy_s"].at[b * 4 + 1])
        sent(g.at[y, z, c, up], S["cy_s"].at[b * 4 + 2])
        sent(g.at[y, z, c, up], S["cy_s"].at[b * 4 + 3])

    @pl.loop(0, 24)
    def _(n):
        sent(yst.at[n], S["yb_s"].at[n])

    @pl.loop(0, 6)
    def _(n):
        sent(zst.at[n], S["zb_s"].at[n])

    @pl.loop(0, 16)
    def _(n):
        sent(own, S["cc_s"].at[n])

    sent(own, S["cz_s"].at[0])
    sent(own, S["cz_s"].at[1])
    sent(g.at[y, z, c, up], S["cz_s"].at[2])
    sent(g.at[y, z, c, up], S["cz_s"].at[3])
    for one in col_moves:
        one.wait_send()
    for one in core_moves:
        one.wait_send()


def shards(residual, enc_weight, enc_bias, dec_weight, dec_bias, target):
    wt = jnp.swapaxes(dec_weight[:, 0], 1, 2)
    vmem = pl.BlockSpec(memory_space=pltpu.VMEM)
    hbm = pl.BlockSpec(memory_space=pl.ANY)
    enc, dec = pl.pallas_call(
        body,
        out_shape=(
            jax.ShapeDtypeStruct((1, 576, 256), BF),
            jax.ShapeDtypeStruct((4, 576, 256), BF),
        ),
        in_specs=[hbm, hbm, vmem, hbm, vmem, vmem],
        out_specs=(vmem, vmem),
        scratch_shapes=[pltpu.VMEM(*spec) for spec in SCRATCH.values()]
        + [pltpu.SemaphoreType.DMA((n,)) for n in SEMS.values()],
        compiler_params=pltpu.CompilerParams(
            collective_id=0, has_side_effects=True, vmem_limit_bytes=56 * 1024 * 1024
        ),
    )(residual, enc_weight, enc_bias, wt, dec_bias, target)
    return enc, jnp.swapaxes(dec, 1, 2)[:, None]


def solution(mesh):
    in_specs = (
        P("layer", "dp", None),
        P("layer", None, "feat"),
        P("layer", "feat"),
        P(None, "layer", "feat", "dp"),
        P("layer", "dp"),
        P("layer", "feat", "dp"),
    )
    out_specs = (P("layer", "dp", "feat"), P(None, "layer", "feat", "dp"))
    return jax.shard_map(shards, mesh=mesh, in_specs=in_specs, out_specs=out_specs, check_vma=False)
```

time: 364 us -> 131 us (0.36)
  the two profiles are of different devices: /device:TPU:6 before, /device:TPU:8 now
where the time goes in v1:
time: 131 us
  Pallas kernels  126 us (96%)
  local copies, waits for them, and re-layouts  4.05 us (3%)
    pallas_call x1, Pallas kernels, shards(): pl.pallas_call(body, out_shape=(jax.ShapeDtypeStruct((1, 576, 256), BF),...  126 us
    unnamed x2, local copies, waits for them, and re-layouts  4.05 us

profile of v1, /device:TPU:8, one launch (start us, length us, event | category | flops | bytes accessed | tf_op | source)
XLA Modules:
  0.0 130.8 jit_solution(4769643757384051135)
XLA Ops:
  0.6 126.1 %shard_map.77 = (bf16[1,576,256]{2,1,0:T(8,128)(2,1)}, bf16[4,576,256]{2,1,0:T(8,128)(2,1)}) custom-call(bf16[1,256,2304]{2,1,0:T(8,128)(2,1)} %refs_0_.1, bf16[1,2304,256]{2,1,0:T(8,128)(2,1)} %refs_1_.1, f32[1,256]{1,0:T(1,128)} %refs_2_.1, bf16[4,576,256]{2,1,0:T(8,128)(2,1)} %bitcast.9, f32[1,576]{1,0:T(1,128)} %refs_4_.1, bf16[1,32,576]{2,1,0:T(8,128)(2,1)} %refs_5_.1), custom_call_target="tpu_custom_call" | custom-call | tf_op jit(solution)/shard_map/pallas_call | solution.py:591
  126.7 1.7 %copy.11 = bf16[1,576,256]{2,1,0:T(8,128)(2,1)} copy(bf16[1,576,256]{2,1,0:T(8,128)(2,1)} %get-tuple-element.10) | data formatting | bytes 589824
  128.4 2.4 %copy.12 = bf16[4,1,256,576]{2,3,1,0:T(8,128)(2,1)} copy(bf16[4,1,256,576]{2,3,1,0:T(8,128)(2,1)} %bitcast.8) | data formatting | bytes 2359296

commit v2 on v0

v2 whole, which is shorter than its diff:
```python
import math

import jax
import jax.numpy as jnp
from jax import lax
from jax.experimental import pallas as pl
from jax.experimental.pallas import tpu as pltpu
from jax.sharding import PartitionSpec as P

MESH = pl.DeviceIdType.MESH
BF = jnp.bfloat16
F32 = jnp.float32
WIN = 640
LAG = 5
WAVES = LAG + 7

SEMS = dict(
    load=3, ar=64, a_right=16, a_left=16, a_n1=16, a_n2=16, a_rl=16,
    rr=4, rr_s=4, rc=3, rc_s=3,
    pc=4, pc_s=4,
    yb=24, yb_s=24, zb=6, zb_s=6,
    cz=4, cz_s=4, cy=16, cy_s=16, cc=16, cc_s=16,
    xr=8, xl=8, xe=8, x_s=24, zc=32, zc_s=16, e=16, e_right=16, e_left=16,
)

SCRATCH = dict(
    resid=((256, 2304), BF), w=((2304, 256), BF), wt=((4, 576, 256), BF),
    pos=((4, 64, 256), F32), codes=((4, 4, 4, 64, 256), BF),
    rw=((4, 256, WIN), BF), rwt=((4, WIN, 256), BF),
    acc=((4, 4, 2, 32, 576), F32), po=((4, 4, 32, 576), BF), pc=((4, 4, 32, 576), BF),
    yst=((24, 16, 576), BF), yb=((24, 16, 576), BF),
    tz=((4, 32, 576), F32), zst=((6, 16, 576), BF), zb=((6, 16, 576), BF),
    g=((4, 4, 2, 32, 576), BF), gt=((4, 576, 256), BF),
    bt=((4, 4, 4, 64, 256), BF), xr=((8, 2, 64, 256), BF), xl=((8, 2, 64, 256), BF), xe=((8, 2, 64, 256), BF),
    s=((8, 2, 64, 256), F32), ss=((16, 64, 256), BF), zc=((32, 64, 256), BF),
    cg=((4, 4, 64, 256), BF), eacc=((WIN, 256), F32),
)


def order(p):
    return jnp.where(p == 0, 0, jnp.where(p == 1, 3, p - 1))


def place(b):
    return jnp.where(b == 0, 0, jnp.where(b == 3, 1, b + 1))


def body(*refs):
    resid_h, w_h, bias, wt_h, dbias, target, enc_o, dec_o = refs[:8]
    R = dict(zip(SCRATCH, refs[8 : 8 + len(SCRATCH)]))
    S = dict(zip(SEMS, refs[8 + len(SCRATCH) :]))
    resid, w, wt, pos, codes = R["resid"], R["w"], R["wt"], R["pos"], R["codes"]
    f = lax.axis_index("feat")
    t = lax.axis_index("layer")
    d = lax.axis_index("dp")
    c, z, y = lax.rem(f, 2), lax.rem(f // 2, 4), f // 8

    def at(yy, zz, core):
        return (lax.rem(yy + 8, 4) * 4 + lax.rem(zz + 8, 4)) * 2 + core

    def along_z(k):
        g = lax.rem(z * 4 + d + k + 16, 16)
        return (at(y, g // 4, c), t, lax.rem(g, 4))

    dev_core = (at(y, z, 1 - c), t, d)
    dev_yp, dev_ym = (at(y + 1, z, c), t, d), (at(y - 1, z, c), t, d)
    dev_zp, dev_zm = (at(y, z + 1, c), t, d), (at(y, z - 1, c), t, d)
    dev_xp, dev_xm = (f, lax.rem(t + 1, 4), d), (f, lax.rem(t + 3, 4), d)
    dev_r, dev_l = (f, t, lax.rem(d + 1, 4)), (f, t, lax.rem(d + 3, 4))
    ym, yp, y2 = lax.rem(y + 3, 4), lax.rem(y + 1, 4), lax.rem(y + 2, 4)
    zm, zp, z2 = lax.rem(z + 3, 4), lax.rem(z + 1, 4), lax.rem(z + 2, 4)
    pd = place(d)

    def copy(src, dst, ssem, rsem, dev):
        return pltpu.make_async_remote_copy(
            src_ref=src, dst_ref=dst, send_sem=ssem, recv_sem=rsem, device_id=dev, device_id_type=MESH
        )

    def arrived(dst, rsem):
        copy(dst, dst, S["load"].at[0], rsem, dev_core).wait_recv()

    def sent(src, ssem):
        copy(src, src, ssem, S["load"].at[0], dev_core).wait_send()

    loads = [
        pltpu.make_async_copy(resid_h.at[0], resid, S["load"].at[0]),
        pltpu.make_async_copy(w_h.at[0], w, S["load"].at[1]),
        pltpu.make_async_copy(wt_h, wt, S["load"].at[2]),
    ]
    for one in loads:
        one.start()

    barrier = pltpu.get_barrier_semaphore()
    partners = [dev_core, dev_yp, dev_ym, dev_zp, dev_zm, dev_xp, dev_xm]
    partners += [along_z(k) for k in (1, -1, 2, -2)]
    for dev in partners:
        pl.semaphore_signal(barrier, inc=1, device_id=dev, device_id_type=MESH)
    pl.semaphore_wait(barrier, len(partners))

    loads[0].wait()
    loads[1].wait()
    pre = jnp.dot(resid[...], w[...], preferred_element_type=F32) + bias[...]
    positive = jnp.maximum(pre, 0.0)
    pos[...] = positive.reshape(4, 64, 256)
    codes[t, :, pd] = (positive * positive).astype(BF).reshape(4, 64, 256)
    loads[2].wait()

    def chunk_z(i):
        return lax.rem(z + jnp.where(i == 0, 2, jnp.where(i == 1, 1, jnp.where(i == 2, 3, 0))), 4)

    def relays(b):
        side = (b == 0) | (b == 3)
        return ((t == 0) & side) | ((t == 2) & jnp.logical_not(side)) | (t == 3)

    relay_from = jnp.where(t == 3, 0, 1)
    dev_relay = (f, jnp.where(t == 3, 2, 3), d)

    def second(b):
        return (t == 0) | ((t == 1) & ((b == 0) | (b == 3)))

    def spread(i, b, fresh):
        p = place(b)
        n = i * 4 + p
        blk = codes.at[t, chunk_z(i), p]
        sem = S["ar"].at[t * 16 + n]

        if not fresh:
            arrived(blk, sem)

        @pl.when((b <= d) & (d < 3))
        def _():
            copy(blk, blk, S["a_right"].at[n], sem, dev_r).start()

        @pl.when((b >= d) & (d > 0))
        def _():
            copy(blk, blk, S["a_left"].at[n], sem, dev_l).start()

        @pl.when(t < 3)
        def _():
            copy(blk, blk, S["a_n1"].at[n], sem, dev_xp).start()

        @pl.when(second(b))
        def _():
            copy(blk, blk, S["a_n2"].at[n], sem, dev_xm).start()

    def relay(i, b):
        @pl.when(relays(b))
        def _():
            p = place(b)
            blk = codes.at[relay_from, chunk_z(i), p]
            sem = S["ar"].at[relay_from * 16 + i * 4 + p]
            arrived(blk, sem)
            copy(blk, blk, S["a_rl"].at[i * 4 + p], sem, dev_relay).start()

    rw, rwt = R["rw"], R["rwt"]

    def start_col(k):
        return pl.multiple_of(k * 576 - 64 * lax.rem(k, 2), 128)

    def move_cols(k, lo, size, slot):
        rows = pl.ds(pl.multiple_of(c * 128 + lo, 64), size)
        dev = along_z(k)
        src = resid.at[rows, pl.ds(start_col(dev[2]), WIN)]
        return copy(src, rw.at[pd, rows], S["rr_s"].at[slot], S["rr"].at[slot], dev)

    col_moves = [move_cols(1, 0, 128, 0), move_cols(-1, 0, 128, 1), move_cols(2, 0, 64, 2), move_cols(-2, 64, 64, 3)]
    half = pl.ds(pl.multiple_of(c * 128, 128), 128)
    other_half = pl.ds(pl.multiple_of((1 - c) * 128, 128), 128)
    slots = [place(lax.rem(d + k, 4)) for k in (3, 1, 2)]
    core_moves = [
        copy(rw.at[k, half], rw.at[k, half], S["rc_s"].at[n], S["rc"].at[n], dev_core) for n, k in enumerate(slots)
    ]

    acc, po, pc = R["acc"], R["po"], R["pc"]

    def recon_chunk(i):
        zz = chunk_z(i)

        @pl.loop(0, 12)
        def _(n):
            l, p = n // 4, lax.rem(n, 4)
            relayed = relays(order(p)) & (l == relay_from)

            @pl.when((l < t) & jnp.logical_not(relayed))
            def _():
                arrived(codes.at[l, zz, p], S["ar"].at[l * 16 + i * 4 + p])

        for top in range(4):
            @pl.when(t == top)
            def _():
                total = None
                for l in range(top + 1):
                    term = lax.dot_general(
                        codes[l, zz].reshape(256, 256), wt[l], (((1,), (1,)), ((), ())), preferred_element_type=F32
                    )
                    total = term if total is None else total + term
                acc[i] = total.reshape(4, 2, 32, 576)

        po[i] = acc[i, :, 1 - c].astype(BF)
        copy(po.at[i], pc.at[i], S["pc_s"].at[i], S["pc"].at[i], dev_core).start()

    yst, yb = R["yst"], R["yb"]

    def partial(i, yy, h):
        rows = pl.ds(16 * h, 16)
        p = place(yy)
        return acc[i, p, c, rows] + pc[i, p, rows].astype(F32)

    def y_send(i, k, value, dev):
        n = i * 6 + k
        yst[n] = value.astype(BF)
        copy(yst.at[n], yb.at[n], S["yb_s"].at[n], S["yb"].at[n], dev).start()

    def y_take(i, k):
        n = i * 6 + k
        arrived(yb.at[n], S["yb"].at[n])
        return yb[n].astype(F32)

    def y_first(i):
        arrived(pc.at[i], S["pc"].at[i])
        y_send(i, 0, partial(i, y2, 0), dev_yp)
        y_send(i, 1, partial(i, y2, 1), dev_ym)
        y_send(i, 2, partial(i, yp, 1), dev_yp)
        y_send(i, 3, partial(i, ym, 0), dev_ym)

    def y_second(i):
        y_send(i, 4, partial(i, yp, 0) + y_take(i, 0), dev_yp)
        y_send(i, 5, partial(i, ym, 1) + y_take(i, 1), dev_ym)

    tz, zst, zb = R["tz"], R["zst"], R["zb"]

    def z_send(k, value, dev):
        zst[k] = value.astype(BF)
        copy(zst.at[k], zb.at[k], S["zb_s"].at[k], S["zb"].at[k], dev).start()

    def z_take(k):
        arrived(zb.at[k], S["zb"].at[k])
        return zb[k].astype(F32)

    def z_first(i):
        top_half = partial(i, y, 0) + y_take(i, 3) + y_take(i, 4)
        low_half = partial(i, y, 1) + y_take(i, 2) + y_take(i, 5)
        tz[i, pl.ds(0, 16)] = top_half
        tz[i, pl.ds(16, 16)] = low_half

        @pl.when(i == 0)
        def _():
            z_send(0, top_half, dev_zp)
            z_send(1, low_half, dev_zm)

        @pl.when(i == 1)
        def _():
            z_send(2, low_half, dev_zp)

        @pl.when(i == 2)
        def _():
            z_send(3, top_half, dev_zm)
            z_send(4, tz[1, pl.ds(0, 16)] + z_take(0), dev_zp)
            z_send(5, tz[2, pl.ds(16, 16)] + z_take(1), dev_zm)

    @pl.loop(0, 4)
    def _(i):
        spread(i, d, True)

    @pl.loop(1, WAVES)
    def _(k):
        @pl.loop(0, 4)
        def _(i):
            h = k - i

            @pl.when((h > 0) & (h < 4))
            def _():
                for b in (d - h, d + h):
                    @pl.when((b >= 0) & (b < 4))
                    def _():
                        spread(i, b, False)

            m = k - 1 - i

            @pl.when((m >= 0) & (m < 4))
            def _():
                @pl.when(d >= m)
                def _():
                    relay(i, d - m)

                @pl.when((m > 0) & (d + m < 4))
                def _():
                    relay(i, d + m)

        @pl.when(k == 6)
        def _():
            for one in col_moves:
                one.start()
            rw[pd] = resid[:, pl.ds(start_col(d), WIN)]

        for lag, step in ((LAG, recon_chunk), (LAG + 1, y_first), (LAG + 2, y_second), (LAG + 3, z_first)):
            @pl.when((k >= lag) & (k < lag + 4))
            def _():
                step(k - lag)

        @pl.when(k == LAG + 3)
        def _():
            arrived(rw.at[slots[0], half], S["rr"].at[0])
            arrived(rw.at[slots[1], half], S["rr"].at[1])
            arrived(rw.at[slots[2], pl.ds(pl.multiple_of(c * 128, 64), 64)], S["rr"].at[2])
            arrived(rw.at[slots[2], pl.ds(pl.multiple_of(c * 128 + 64, 64), 64)], S["rr"].at[3])
            for one in core_moves:
                one.start()

    scale = 1.0 / math.sqrt(1024)
    g = R["g"]
    py = place(y)
    for h, ks in enumerate(((3, 4), (2, 5))):
        rows = pl.ds(16 * h, 16)
        recon = tz[3, rows] + z_take(ks[0]) + z_take(ks[1])
        err = recon + dbias[...] - target[0, rows].astype(F32)
        g[z, py, c, rows] = (err * scale).astype(BF)

    up, down = pl.ds(0, 16), pl.ds(16, 16)

    def block_z(j):
        return lax.rem(z + jnp.where(j == 0, 0, jnp.where(j == 1, 3, jnp.where(j == 2, 1, 2))), 4)

    def to_core(yy, j):
        n = j * 4 + place(yy)
        blk = g.at[block_z(j), place(yy), c]
        copy(blk, blk, S["cc_s"].at[n], S["cc"].at[n], dev_core).start()

    def to_y(j):
        blk = g.at[block_z(j), py, c]
        copy(blk, blk, S["cy_s"].at[j * 4], S["cy"].at[j * 4], dev_yp).start()
        copy(blk, blk, S["cy_s"].at[j * 4 + 1], S["cy"].at[j * 4 + 1], dev_ym).start()
        to_core(y, j)

    def y_forward(j):
        blk = g.at[block_z(j), place(ym), c]
        arrived(blk, S["cy"].at[j * 4])
        part = g.at[block_z(j), place(ym), c, up]
        copy(part, part, S["cy_s"].at[j * 4 + 2], S["cy"].at[j * 4 + 2], dev_yp).start()
        to_core(ym, j)
        blk = g.at[block_z(j), place(yp), c]
        arrived(blk, S["cy"].at[j * 4 + 1])
        part = g.at[block_z(j), place(yp), c, down]
        copy(part, part, S["cy_s"].at[j * 4 + 3], S["cy"].at[j * 4 + 3], dev_ym).start()
        to_core(yp, j)

    def y_last(j):
        arrived(g.at[block_z(j), place(y2), c, up], S["cy"].at[j * 4 + 2])
        arrived(g.at[block_z(j), place(y2), c, down], S["cy"].at[j * 4 + 3])
        to_core(y2, j)

    bt, xr, xl, xe, s, ss, zc = R["bt"], R["xr"], R["xl"], R["xe"], R["s"], R["ss"], R["zc"]
    gt, cg, eacc = R["gt"], R["cg"], R["eacc"]

    def x_send(k, u, l, dst, name, dev):
        src = bt.at[l, u // 2, pl.ds(2 * lax.rem(u, 2), 2)]
        copy(src, dst.at[u], S["x_s"].at[k * 8 + u], S[name].at[u], dev).start()

    def back(j):
        zz = block_z(j)

        @pl.loop(0, 4)
        def _(p):
            arrived(g.at[zz, p, 1 - c], S["cc"].at[j * 4 + p])

        @pl.loop(0, t + 1)
        def _(l):
            term = jnp.dot(g[zz].reshape(256, 576), wt[l], preferred_element_type=F32)
            bt[l, j] = term.astype(BF).reshape(4, 64, 256)

        for h in range(2):
            u = j * 2 + h

            @pl.when(t == 1)
            def _():
                x_send(0, u, 0, xr, "xr", dev_xm)

            @pl.when(t == 2)
            def _():
                x_send(0, u, 0, xl, "xl", dev_xp)
                if h == 0:
                    x_send(1, u, 1, xr, "xr", dev_xm)

            @pl.when(t == 3)
            def _():
                x_send(1, u, 1, xe, "xe", dev_xp if h == 0 else dev_xm)
                x_send(2, u, 2, xr, "xr", dev_xm)

    def add_in(l, u, other, name):
        arrived(other.at[u], S[name].at[u])
        j, part = u // 2, pl.ds(2 * lax.rem(u, 2), 2)
        bt[l, j, part] = (bt[l, j, part].astype(F32) + other[u].astype(F32)).astype(BF)

    def x_second(u):
        h = lax.rem(u, 2)

        @pl.when(t == 3)
        def _():
            add_in(0, u, xl, "xl")
            x_send(0, u, 0, xl, "xl", dev_xp)

        @pl.when((t == 2) & (h == 1))
        def _():
            add_in(1, u, xe, "xe")
            x_send(1, u, 1, xr, "xr", dev_xm)

        @pl.when((t == 0) & (h == 0))
        def _():
            arrived(xe.at[u], S["xe"].at[u])
            copy(xe.at[u], xl.at[u], S["x_s"].at[u], S["xl"].at[u], dev_xp).start()

    def chain(u, pos_in_line):
        @pl.loop(0, 2)
        def _(r):
            p = 2 * lax.rem(u, 2) + r
            n = (u // 2) * 4 + p
            q = order(p)
            rightward = (d == pos_in_line) & (q > pos_in_line)
            leftward = (d == 3 - pos_in_line) & (q < 3 - pos_in_line)
            for going, base, dev in ((rightward, 0, dev_r), (leftward, 16, dev_l)):
                @pl.when(going)
                def _():
                    value = s[u, r]
                    if pos_in_line > 0:
                        arrived(zc.at[base + n], S["zc"].at[base + n])
                        value = value + zc[base + n].astype(F32)
                    ss[n] = value.astype(BF)
                    copy(ss.at[n], zc.at[base + n], S["zc_s"].at[n], S["zc"].at[base + n], dev).start()

    def x_sum(u):
        h = lax.rem(u, 2)
        s[u] = bt[t, u // 2, pl.ds(2 * h, 2)].astype(F32)

        @pl.when(t < 3)
        def _():
            arrived(xr.at[u], S["xr"].at[u])
            s[u] += xr[u].astype(F32)

        @pl.when((t == 0) | ((t == 1) & (h == 0)))
        def _():
            arrived(xl.at[u], S["xl"].at[u])
            s[u] += xl[u].astype(F32)

        chain(u, 0)

    def final(u):
        @pl.when(pd // 2 == lax.rem(u, 2))
        def _():
            r = lax.rem(pd, 2)
            j = u // 2
            n = j * 4 + pd

            @pl.when(d > 0)
            def _():
                arrived(zc.at[n], S["zc"].at[n])
                s[u, r] += zc[n].astype(F32)

            @pl.when(d < 3)
            def _():
                arrived(zc.at[16 + n], S["zc"].at[16 + n])
                s[u, r] += zc[16 + n].astype(F32)

            cg[j, pd] = (s[u, r] * 2.0 * pos[block_z(j)]).astype(BF)
            blk, sem = cg.at[j, pd], S["e"].at[n]

            @pl.when(d < 3)
            def _():
                copy(blk, blk, S["e_right"].at[n], sem, dev_r).start()

            @pl.when(d > 0)
            def _():
                copy(blk, blk, S["e_left"].at[n], sem, dev_l).start()

    def gather(u, hops):
        @pl.loop(0, 2)
        def _(r):
            p = 2 * lax.rem(u, 2) + r
            n = (u // 2) * 4 + p
            q = order(p)
            blk, sem = cg.at[u // 2, p], S["e"].at[n]

            @pl.when((q == d - hops) | (q == d + hops))
            def _():
                arrived(blk, sem)

            @pl.when((q == d - hops) & (d < 3))
            def _():
                copy(blk, blk, S["e_right"].at[n], sem, dev_r).start()

            @pl.when((q == d + hops) & (d > 0))
            def _():
                copy(blk, blk, S["e_left"].at[n], sem, dev_l).start()

    def dec_grad(i):
        @pl.when(i <= t)
        def _():
            total = None
            for k in range(4):
                term = jnp.dot(gt[k], codes[i, k].reshape(256, 256), preferred_element_type=F32)
                total = term if total is None else total + term
            dec_o[i] = total.astype(BF)

        @pl.when(i > t)
        def _():
            dec_o[i] = jnp.zeros((576, 256), BF)

    own = g.at[z, py, c]
    copy(own, own, S["cz_s"].at[0], S["cz"].at[0], dev_zp).start()
    copy(own, own, S["cz_s"].at[1], S["cz"].at[1], dev_zm).start()
    to_y(0)
    for n, k in enumerate(slots):
        arrived(rw.at[k, other_half], S["rc"].at[n])

    @pl.loop(0, 4)
    def _(j):
        rwt[j] = rw[:, pl.ds(pl.multiple_of(64 * block_z(j), 64), 64)].reshape(256, WIN).T

    eacc[...] = jnp.zeros_like(eacc)
    y_forward(0)
    arrived(g.at[zm, py, c], S["cz"].at[0])
    part = g.at[zm, py, c, up]
    copy(part, part, S["cz_s"].at[2], S["cz"].at[2], dev_zp).start()
    to_y(1)
    arrived(g.at[zp, py, c], S["cz"].at[1])
    part = g.at[zp, py, c, down]
    copy(part, part, S["cz_s"].at[3], S["cz"].at[3], dev_zm).start()
    to_y(2)
    y_last(0)
    back(0)

    @pl.loop(0, 17)
    def _(k):
        @pl.when(k == 0)
        def _():
            y_forward(1)
            y_forward(2)
            arrived(g.at[z2, py, c, up], S["cz"].at[2])
            arrived(g.at[z2, py, c, down], S["cz"].at[3])
            to_y(3)
            y_last(1)
            back(1)

        @pl.when(k == 1)
        def _():
            y_last(2)
            back(2)

        @pl.when(k == 2)
        def _():
            y_forward(3)

        @pl.when(k == 3)
        def _():
            y_last(3)
            back(3)

        def stage(lag, step, *more):
            @pl.when((k >= lag) & (k < lag + 8))
            def _():
                step(k - lag, *more)

        stage(1, x_second)
        stage(3, x_sum)

        @pl.when((k >= 4) & (k < 8))
        def _():
            q = k - 4
            gt[q] = g[q].reshape(256, 576).T

        stage(4, chain, 1)
        stage(5, chain, 2)
        stage(6, final)
        stage(7, gather, 1)
        stage(8, gather, 2)
        stage(9, gather, 3)

        @pl.when((k >= 8) & (k < 12))
        def _():
            dec_grad(k - 8)

        @pl.when((k >= 10) & (lax.rem(k, 2) == 0))
        def _():
            j = (k - 10) // 2
            eacc[...] += jnp.dot(rwt[j], cg[j].reshape(256, 256), preferred_element_type=F32)

    shift = pl.multiple_of(64 * lax.rem(d, 2), 64)
    enc_o[0] = eacc[pl.ds(shift, 576)].astype(BF)

    @pl.loop(0, 16)
    def _(n):
        p = lax.rem(n, 4)
        b = order(p)
        blk = ss.at[n]

        @pl.when((b <= d) & (d < 3))
        def _():
            sent(blk, S["a_right"].at[n])
            sent(blk, S["e_right"].at[n])

        @pl.when((b >= d) & (d > 0))
        def _():
            sent(blk, S["a_left"].at[n])
            sent(blk, S["e_left"].at[n])

        @pl.when(t < 3)
        def _():
            sent(blk, S["a_n1"].at[n])

        @pl.when(second(b))
        def _():
            sent(blk, S["a_n2"].at[n])

        @pl.when(relays(b))
        def _():
            sent(blk, S["a_rl"].at[n])

        @pl.when(d != b)
        def _():
            sent(blk, S["zc_s"].at[n])

        sent(own, S["cc_s"].at[n])

    @pl.loop(0, 8)
    def _(u):
        @pl.when((t > 0) | (lax.rem(u, 2) == 0))
        def _():
            sent(xr.at[u], S["x_s"].at[u])

        @pl.when(t >= 2)
        def _():
            sent(xr.at[u], S["x_s"].at[8 + u])

        @pl.when(t == 3)
        def _():
            sent(xr.at[u], S["x_s"].at[16 + u])

    @pl.loop(0, 4)
    def _(j):
        sent(po.at[j], S["pc_s"].at[j])
        sent(own, S["cy_s"].at[j * 4])
        sent(own, S["cy_s"].at[j * 4 + 1])
        sent(zst.at[0], S["cy_s"].at[j * 4 + 2])
        sent(zst.at[0], S["cy_s"].at[j * 4 + 3])

    @pl.loop(0, 24)
    def _(n):
        sent(yst.at[n], S["yb_s"].at[n])

    @pl.loop(0, 6)
    def _(n):
        sent(zst.at[n], S["zb_s"].at[n])

    sent(own, S["cz_s"].at[0])
    sent(own, S["cz_s"].at[1])
    sent(zst.at[0], S["cz_s"].at[2])
    sent(zst.at[0], S["cz_s"].at[3])
    for one in col_moves:
        one.wait_send()
    for one in core_moves:
        one.wait_send()


def shards(residual, enc_weight, enc_bias, dec_weight, dec_bias, target):
    wt = jnp.swapaxes(dec_weight[:, 0], 1, 2)
    vmem = pl.BlockSpec(memory_space=pltpu.VMEM)
    hbm = pl.BlockSpec(memory_space=pl.ANY)
    enc, dec = pl.pallas_call(
        body,
        out_shape=(
            jax.ShapeDtypeStruct((1, 576, 256), BF),
            jax.ShapeDtypeStruct((4, 576, 256), BF),
        ),
        in_specs=[hbm, hbm, vmem, hbm, vmem, vmem],
        out_specs=(vmem, vmem),
        scratch_shapes=[pltpu.VMEM(*spec) for spec in SCRATCH.values()]
        + [pltpu.SemaphoreType.DMA((n,)) for n in SEMS.values()],
        compiler_params=pltpu.CompilerParams(
            collective_id=0, has_side_effects=True, vmem_limit_bytes=56 * 1024 * 1024
        ),
    )(residual, enc_weight, enc_bias, wt, dec_bias, target)
    return enc, jnp.swapaxes(dec, 1, 2)[:, None]


def solution(mesh):
    in_specs = (
        P("layer", "dp", None),
        P("layer", None, "feat"),
        P("layer", "feat"),
        P(None, "layer", "feat", "dp"),
        P("layer", "dp"),
        P("layer", "feat", "dp"),
    )
    out_specs = (P("layer", "dp", "feat"), P(None, "layer", "feat", "dp"))
    return jax.shard_map(shards, mesh=mesh, in_specs=in_specs, out_specs=out_specs, check_vma=False)
```

time: 364 us -> 123 us (0.34)
  waiting for transfers between devices: 258 us -> 0 us
  Pallas kernels: 0 us -> 117 us
  blocking collectives: 54.3 us -> 0 us
  between operations: 14.1 us -> 0.64 us
  matrix products: 13.1 us -> 0 us
  starting transfers between devices: 13 us -> 0 us
    reduce_scatter x1 -> x0, waiting for transfers between devices: 117 us -> none  [shards(): lax.psum_scatter(jnp.einsum('lnf,lfd->nd', codes_all, weights, preferred_...]
    pallas_call x0 -> x1, Pallas kernels: none -> 117 us  [shards(): pl.pallas_call(body, out_shape=(jax.ShapeDtypeStruct((1, 576, 256), BF),...]
    all_to_all x2 -> x0, waiting for transfers between devices: 70.8 us -> none  [the longest x1 47.3 us: copy_for_each(): return lax.all_to_all(copies, axis, split_axis=0, concat_axis=0, tiled=True)]
    all_gather x1 -> x0, waiting for transfers between devices: 70 us -> none  [shards(): grad_all = lax.all_gather(grad_rows, 'feat', axis=0, tiled=True)]
    all_to_all x1 -> x0, blocking collectives: 54.3 us -> none  [summed_on_arrival(): parts = lax.all_to_all(split_up(value, dim, count), axis, 0, 0, tiled=True)]
    dot_general x5 -> x0, matrix products: 13.1 us -> none  [the longest x1 4.4 us: shards(): jnp.einsum('lnf,nd->lfd', codes_all, grad_all, preferred_element_type=jnp...]
    all_to_all x2 -> x0, starting transfers between devices: 13 us -> none  [the longest x1 9.43 us: copy_for_each(): return lax.all_to_all(copies, axis, split_axis=0, concat_axis=0, tiled=True)]
  transfers between devices with their start and end apart: 4 -> 0, of which waited for: 4 -> 0; matrix products, arithmetic and copies ran while one was open for 1% -> 0% of each run, Pallas kernels for 0% -> 0%
where the time goes in v2:
time: 123 us; the launch traced here: 121 us
  Pallas kernels  117 us (95%)
  local copies, waits for them, and re-layouts  4.05 us (3%)
    pallas_call x1, Pallas kernels, shards(): pl.pallas_call(body, out_shape=(jax.ShapeDtypeStruct((1, 576, 256), BF),...  117 us
    unnamed x2, local copies, waits for them, and re-layouts  4.05 us

profile of v2, /device:TPU:6, one launch (start us, length us, event | category | flops | bytes accessed | tf_op | source)
XLA Modules:
  0.0 121.3 jit_solution(6071301979587316195)
XLA Ops:
  0.6 116.7 %shard_map.77 = (bf16[1,576,256]{2,1,0:T(8,128)(2,1)}, bf16[4,576,256]{2,1,0:T(8,128)(2,1)}) custom-call(bf16[1,256,2304]{2,1,0:T(8,128)(2,1)} %refs_0_.1, bf16[1,2304,256]{2,1,0:T(8,128)(2,1)} %refs_1_.1, f32[1,256]{1,0:T(1,128)} %refs_2_.1, bf16[4,576,256]{2,1,0:T(8,128)(2,1)} %bitcast.9, f32[1,576]{1,0:T(1,128)} %refs_4_.1, bf16[1,32,576]{2,1,0:T(8,128)(2,1)} %refs_5_.1), custom_call_target="tpu_custom_call" | custom-call | tf_op jit(solution)/shard_map/pallas_call | solution.py:667
  117.3 1.7 %copy.11 = bf16[1,576,256]{2,1,0:T(8,128)(2,1)} copy(bf16[1,576,256]{2,1,0:T(8,128)(2,1)} %get-tuple-element.10) | data formatting | bytes 589824
  119.0 2.4 %copy.12 = bf16[4,1,256,576]{2,3,1,0:T(8,128)(2,1)} copy(bf16[4,1,256,576]{2,3,1,0:T(8,128)(2,1)} %bitcast.8) | data formatting | bytes 2359296

commit v3 on v2

v3 whole, which is shorter than its diff:
```python
import math

import jax
import jax.numpy as jnp
from jax import lax
from jax.experimental import pallas as pl
from jax.experimental.pallas import tpu as pltpu
from jax.sharding import PartitionSpec as P

MESH = pl.DeviceIdType.MESH
BF = jnp.bfloat16
F32 = jnp.float32
WIN = 640

SEMS = dict(
    load=3, ar=64, az=12, a_n1=16, a_n2=16, a_rl=16,
    rr=4, rr_s=4, rc=3, rc_s=3,
    pc=4, pc_s=4,
    yb=12, yb_s=12, zb=3, zb_s=3,
    cz=3, cz_s=3, cy=12, cy_s=12, cc=4, cc_s=4,
    xr=8, xl=8, xe=8, x_s=24, zc=64, zc_s=16, e=16, e_s=12,
)

SCRATCH = dict(
    resid=((256, 2304), BF), w=((2304, 256), BF), wt=((4, 576, 256), BF),
    pos=((4, 64, 256), F32), codes=((4, 4, 4, 64, 256), BF),
    rw=((4, 256, WIN), BF), rwt=((4, WIN, 256), BF),
    acc=((4, 4, 2, 32, 576), F32), po=((4, 4, 32, 576), BF), pc=((4, 4, 32, 576), BF),
    yst=((12, 32, 576), BF), yb=((12, 32, 576), BF),
    tz=((32, 576), F32), zst=((3, 32, 576), BF), zb=((3, 32, 576), BF),
    g=((4, 4, 2, 32, 576), BF), gt=((4, 576, 256), BF),
    bt=((4, 4, 4, 64, 256), BF), xr=((8, 2, 64, 256), BF), xl=((8, 2, 64, 256), BF), xe=((8, 2, 64, 256), BF),
    s=((8, 2, 64, 256), F32), ss=((16, 64, 256), BF), zc=((4, 16, 64, 256), BF),
    cg=((4, 4, 64, 256), BF), eacc=((WIN, 256), F32),
)


def order(p):
    return jnp.where(p == 0, 0, jnp.where(p == 1, 3, p - 1))


def place(b):
    return jnp.where(b == 0, 0, jnp.where(b == 3, 1, b + 1))


def body(*refs):
    resid_h, w_h, bias, wt_h, dbias, target, enc_o, dec_o = refs[:8]
    R = dict(zip(SCRATCH, refs[8 : 8 + len(SCRATCH)]))
    S = dict(zip(SEMS, refs[8 + len(SCRATCH) :]))
    resid, w, wt, pos, codes = R["resid"], R["w"], R["wt"], R["pos"], R["codes"]
    f = lax.axis_index("feat")
    t = lax.axis_index("layer")
    d = lax.axis_index("dp")
    c, z, y = lax.rem(f, 2), lax.rem(f // 2, 4), f // 8

    def at(yy, zz, core):
        return (lax.rem(yy + 8, 4) * 4 + lax.rem(zz + 8, 4)) * 2 + core

    def along_z(k):
        g = lax.rem(z * 4 + d + k + 16, 16)
        return (at(y, g // 4, c), t, lax.rem(g, 4))

    dev_core = (at(y, z, 1 - c), t, d)
    dev_yp, dev_ym = (at(y + 1, z, c), t, d), (at(y - 1, z, c), t, d)
    dev_zp, dev_zm = (at(y, z + 1, c), t, d), (at(y, z - 1, c), t, d)
    dev_xp, dev_xm = (f, lax.rem(t + 1, 4), d), (f, lax.rem(t + 3, 4), d)
    dev_z2, dev_y2 = (at(y, z + 2, c), t, d), (at(y + 2, z, c), t, d)
    others = [(f, t, lax.rem(d + k, 4)) for k in (1, 2, 3)]
    ym, yp, y2 = lax.rem(y + 3, 4), lax.rem(y + 1, 4), lax.rem(y + 2, 4)
    zm, zp, z2 = lax.rem(z + 3, 4), lax.rem(z + 1, 4), lax.rem(z + 2, 4)
    pd = place(d)

    def copy(src, dst, ssem, rsem, dev):
        return pltpu.make_async_remote_copy(
            src_ref=src, dst_ref=dst, send_sem=ssem, recv_sem=rsem, device_id=dev, device_id_type=MESH
        )

    def arrived(dst, rsem):
        copy(dst, dst, S["load"].at[0], rsem, dev_core).wait_recv()

    def sent(src, ssem):
        copy(src, src, ssem, S["load"].at[0], dev_core).wait_send()

    loads = [
        pltpu.make_async_copy(resid_h.at[0], resid, S["load"].at[0]),
        pltpu.make_async_copy(w_h.at[0], w, S["load"].at[1]),
        pltpu.make_async_copy(wt_h, wt, S["load"].at[2]),
    ]
    for one in loads:
        one.start()

    barrier = pltpu.get_barrier_semaphore()
    partners = [dev_core, dev_yp, dev_ym, dev_zp, dev_zm, dev_xp, dev_xm]
    partners += [dev_y2, dev_z2] + others + [along_z(k) for k in (1, -1, 2, -2)]
    for dev in partners:
        pl.semaphore_signal(barrier, inc=1, device_id=dev, device_id_type=MESH)
    pl.semaphore_wait(barrier, len(partners))

    loads[0].wait()
    loads[1].wait()
    pre = jnp.dot(resid[...], w[...], preferred_element_type=F32) + bias[...]
    positive = jnp.maximum(pre, 0.0)
    pos[...] = positive.reshape(4, 64, 256)
    codes[t, :, pd] = (positive * positive).astype(BF).reshape(4, 64, 256)
    loads[2].wait()

    def chunk_z(i):
        return lax.rem(z + jnp.where(i == 0, 2, jnp.where(i == 1, 1, jnp.where(i == 2, 3, 0))), 4)

    def relays(b):
        side = (b == 0) | (b == 3)
        return ((t == 0) & side) | ((t == 2) & jnp.logical_not(side)) | (t == 3)

    relay_from = jnp.where(t == 3, 0, 1)
    dev_relay = (f, jnp.where(t == 3, 2, 3), d)

    def second(b):
        return (t == 0) | ((t == 1) & ((b == 0) | (b == 3)))

    def to_line(i):
        blk = codes.at[t, chunk_z(i), pd]
        for k, dev in enumerate(others):
            copy(blk, blk, S["az"].at[i * 3 + k], S["ar"].at[t * 16 + i * 4 + pd], dev).start()

    def to_layers(i, b):
        p = place(b)
        n = i * 4 + p
        blk = codes.at[t, chunk_z(i), p]
        sem = S["ar"].at[t * 16 + n]

        @pl.when(t < 3)
        def _():
            copy(blk, blk, S["a_n1"].at[n], sem, dev_xp).start()

        @pl.when(second(b))
        def _():
            copy(blk, blk, S["a_n2"].at[n], sem, dev_xm).start()

    def relay(i, b):
        @pl.when(relays(b))
        def _():
            p = place(b)
            blk = codes.at[relay_from, chunk_z(i), p]
            sem = S["ar"].at[relay_from * 16 + i * 4 + p]
            arrived(blk, sem)
            copy(blk, blk, S["a_rl"].at[i * 4 + p], sem, dev_relay).start()

    rw, rwt = R["rw"], R["rwt"]

    def start_col(k):
        return pl.multiple_of(k * 576 - 64 * lax.rem(k, 2), 128)

    def move_cols(k, lo, size, slot):
        rows = pl.ds(pl.multiple_of(c * 128 + lo, 64), size)
        dev = along_z(k)
        src = resid.at[rows, pl.ds(start_col(dev[2]), WIN)]
        return copy(src, rw.at[pd, rows], S["rr_s"].at[slot], S["rr"].at[slot], dev)

    col_moves = [move_cols(1, 0, 128, 0), move_cols(-1, 0, 128, 1), move_cols(2, 0, 64, 2), move_cols(-2, 64, 64, 3)]
    half = pl.ds(pl.multiple_of(c * 128, 128), 128)
    other_half = pl.ds(pl.multiple_of((1 - c) * 128, 128), 128)
    slots = [place(lax.rem(d + k, 4)) for k in (3, 1, 2)]
    core_moves = [
        copy(rw.at[k, half], rw.at[k, half], S["rc_s"].at[n], S["rc"].at[n], dev_core) for n, k in enumerate(slots)
    ]

    acc, po, pc = R["acc"], R["po"], R["pc"]

    def recon_chunk(i):
        zz = chunk_z(i)

        @pl.loop(0, 12)
        def _(n):
            l, p = n // 4, lax.rem(n, 4)
            relayed = relays(order(p)) & (l == relay_from)

            @pl.when((l < t) & jnp.logical_not(relayed))
            def _():
                arrived(codes.at[l, zz, p], S["ar"].at[l * 16 + i * 4 + p])

        for top in range(4):
            @pl.when(t == top)
            def _():
                total = None
                for l in range(top + 1):
                    term = lax.dot_general(
                        codes[l, zz].reshape(256, 256), wt[l], (((1,), (1,)), ((), ())), preferred_element_type=F32
                    )
                    total = term if total is None else total + term
                acc[i] = total.reshape(4, 2, 32, 576)

        po[i] = acc[i, :, 1 - c].astype(BF)
        copy(po.at[i], pc.at[i], S["pc_s"].at[i], S["pc"].at[i], dev_core).start()

    yst, yb = R["yst"], R["yb"]

    def partial(i, yy):
        p = place(yy)
        return acc[i, p, c] + pc[i, p].astype(F32)

    def y_part(i):
        arrived(pc.at[i], S["pc"].at[i])
        for k, (yy, dev) in enumerate(((yp, dev_yp), (ym, dev_ym), (y2, dev_y2))):
            n = i * 3 + k
            yst[n] = partial(i, yy).astype(BF)
            copy(yst.at[n], yb.at[n], S["yb_s"].at[n], S["yb"].at[n], dev).start()

    tz, zst, zb = R["tz"], R["zst"], R["zb"]

    def z_part(i):
        total = partial(i, y)
        for k in range(3):
            n = i * 3 + k
            arrived(yb.at[n], S["yb"].at[n])
            total = total + yb[n].astype(F32)
        tz[...] = total

        for k, dev in enumerate((dev_z2, dev_zp, dev_zm)):
            @pl.when(i == k)
            def _():
                zst[k] = total.astype(BF)
                copy(zst.at[k], zb.at[k], S["zb_s"].at[k], S["zb"].at[k], dev).start()

    for i in range(4):
        to_line(i)
    for i in range(2):
        to_layers(i, d)

    @pl.loop(0, 8)
    def _(k):
        @pl.when((k >= 4) & (k < 8))
        def _():
            z_part(k - 4)

        @pl.when((k >= 3) & (k < 7))
        def _():
            y_part(k - 3)

        @pl.when(k < 4)
        def _():
            for h in range(1, 4):
                for b in (d - h, d + h):
                    @pl.when((b >= 0) & (b < 4))
                    def _():
                        p = place(b)
                        arrived(codes.at[t, chunk_z(k), p], S["ar"].at[t * 16 + k * 4 + p])
                        to_layers(k, b)

        @pl.when(k < 2)
        def _():
            to_layers(k + 2, d)

        @pl.when((k >= 1) & (k < 5))
        def _():
            relay(k - 1, d)
            for h in range(1, 4):
                for b in (d - h, d + h):
                    @pl.when((b >= 0) & (b < 4))
                    def _():
                        relay(k - 1, b)

        @pl.when((k >= 2) & (k < 6))
        def _():
            recon_chunk(k - 2)

        @pl.when(k == 3)
        def _():
            for one in col_moves:
                one.start()
            rw[pd] = resid[:, pl.ds(start_col(d), WIN)]

        @pl.when(k == 6)
        def _():
            arrived(rw.at[slots[0], half], S["rr"].at[0])
            arrived(rw.at[slots[1], half], S["rr"].at[1])
            arrived(rw.at[slots[2], pl.ds(pl.multiple_of(c * 128, 64), 64)], S["rr"].at[2])
            arrived(rw.at[slots[2], pl.ds(pl.multiple_of(c * 128 + 64, 64), 64)], S["rr"].at[3])
            for one in core_moves:
                one.start()

    scale = 1.0 / math.sqrt(1024)
    g = R["g"]
    py = place(y)
    recon = tz[...]
    for k in range(3):
        arrived(zb.at[k], S["zb"].at[k])
        recon = recon + zb[k].astype(F32)
    g[z, py, c] = ((recon + dbias[...] - target[0].astype(F32)) * scale).astype(BF)

    def block_z(j):
        return lax.rem(z + jnp.where(j == 0, 0, jnp.where(j == 1, 3, jnp.where(j == 2, 1, 2))), 4)

    def to_y(j):
        blk = g.at[block_z(j), py, c]
        for k, dev in enumerate((dev_yp, dev_ym, dev_y2)):
            copy(blk, blk, S["cy_s"].at[j * 3 + k], S["cy"].at[j * 3 + k], dev).start()

    def from_z(j):
        arrived(g.at[block_z(j), py, c], S["cz"].at[j - 1])
        to_y(j)

    def from_y(j):
        for k, yy in enumerate((ym, yp, y2)):
            arrived(g.at[block_z(j), place(yy), c], S["cy"].at[j * 3 + k])
        blk = g.at[block_z(j), :, c]
        copy(blk, blk, S["cc_s"].at[j], S["cc"].at[j], dev_core).start()

    bt, xr, xl, xe, s, ss, zc = R["bt"], R["xr"], R["xl"], R["xe"], R["s"], R["ss"], R["zc"]
    gt, cg, eacc = R["gt"], R["cg"], R["eacc"]

    def x_send(k, u, l, dst, name, dev):
        src = bt.at[l, u // 2, pl.ds(2 * lax.rem(u, 2), 2)]
        copy(src, dst.at[u], S["x_s"].at[k * 8 + u], S[name].at[u], dev).start()

    def back(j):
        zz = block_z(j)

        arrived(g.at[zz, :, 1 - c], S["cc"].at[j])

        @pl.loop(0, t + 1)
        def _(l):
            term = jnp.dot(g[zz].reshape(256, 576), wt[l], preferred_element_type=F32)
            bt[l, j] = term.astype(BF).reshape(4, 64, 256)

        for h in range(2):
            u = j * 2 + h

            @pl.when(t == 1)
            def _():
                x_send(0, u, 0, xr, "xr", dev_xm)

            @pl.when(t == 2)
            def _():
                x_send(0, u, 0, xl, "xl", dev_xp)
                if h == 0:
                    x_send(1, u, 1, xr, "xr", dev_xm)

            @pl.when(t == 3)
            def _():
                x_send(1, u, 1, xe, "xe", dev_xp if h == 0 else dev_xm)
                x_send(2, u, 2, xr, "xr", dev_xm)

    def add_in(l, u, other, name):
        arrived(other.at[u], S[name].at[u])
        j, part = u // 2, pl.ds(2 * lax.rem(u, 2), 2)
        bt[l, j, part] = (bt[l, j, part].astype(F32) + other[u].astype(F32)).astype(BF)

    def x_second(u):
        h = lax.rem(u, 2)

        @pl.when(t == 3)
        def _():
            add_in(0, u, xl, "xl")
            x_send(0, u, 0, xl, "xl", dev_xp)

        @pl.when((t == 2) & (h == 1))
        def _():
            add_in(1, u, xe, "xe")
            x_send(1, u, 1, xr, "xr", dev_xm)

        @pl.when((t == 0) & (h == 0))
        def _():
            arrived(xe.at[u], S["xe"].at[u])
            copy(xe.at[u], xl.at[u], S["x_s"].at[u], S["xl"].at[u], dev_xp).start()

    def x_sum(u):
        h = lax.rem(u, 2)
        s[u] = bt[t, u // 2, pl.ds(2 * h, 2)].astype(F32)

        @pl.when(t < 3)
        def _():
            arrived(xr.at[u], S["xr"].at[u])
            s[u] += xr[u].astype(F32)

        @pl.when((t == 0) | ((t == 1) & (h == 0)))
        def _():
            arrived(xl.at[u], S["xl"].at[u])
            s[u] += xl[u].astype(F32)

        @pl.loop(0, 2)
        def _(r):
            p = 2 * h + r
            n = (u // 2) * 4 + p
            q = order(p)

            @pl.when(q != d)
            def _():
                ss[n] = s[u, r].astype(BF)
                copy(ss.at[n], zc.at[d, n], S["zc_s"].at[n], S["zc"].at[d * 16 + n], (f, t, q)).start()

    def final(u):
        @pl.when(pd // 2 == lax.rem(u, 2))
        def _():
            j = u // 2
            n = j * 4 + pd
            total = s[u, lax.rem(pd, 2)]
            for k in (1, 3, 2):
                q = lax.rem(d + k, 4)
                arrived(zc.at[q, n], S["zc"].at[q * 16 + n])
                total = total + zc[q, n].astype(F32)

            cg[j, pd] = (total * 2.0 * pos[block_z(j)]).astype(BF)
            blk = cg.at[j, pd]
            for k, dev in enumerate(others):
                copy(blk, blk, S["e_s"].at[j * 3 + k], S["e"].at[n], dev).start()

    def gather(u):
        @pl.loop(0, 2)
        def _(r):
            p = 2 * lax.rem(u, 2) + r

            @pl.when(p != pd)
            def _():
                arrived(cg.at[u // 2, p], S["e"].at[(u // 2) * 4 + p])

    def dec_grad(i):
        @pl.when(i <= t)
        def _():
            total = None
            for k in range(4):
                term = jnp.dot(gt[k], codes[i, k].reshape(256, 256), preferred_element_type=F32)
                total = term if total is None else total + term
            dec_o[i] = total.astype(BF)

        @pl.when(i > t)
        def _():
            dec_o[i] = jnp.zeros((576, 256), BF)

    own = g.at[z, py, c]
    for k, dev in enumerate((dev_zp, dev_zm, dev_z2)):
        copy(own, own, S["cz_s"].at[k], S["cz"].at[k], dev).start()
    to_y(0)
    for n, k in enumerate(slots):
        arrived(rw.at[k, other_half], S["rc"].at[n])

    @pl.loop(0, 4)
    def _(j):
        rwt[j] = rw[:, pl.ds(pl.multiple_of(64 * block_z(j), 64), 64)].reshape(256, WIN).T

    eacc[...] = jnp.zeros_like(eacc)
    from_y(0)
    from_z(1)
    from_z(2)
    back(0)
    from_z(3)
    from_y(1)
    from_y(2)
    back(1)

    @pl.loop(0, 14)
    def _(k):
        def stage(lag, step):
            @pl.when((k >= lag) & (k < lag + 8))
            def _():
                step(k - lag)

        stage(6, gather)

        @pl.when((k >= 7) & (lax.rem(k, 2) == 1))
        def _():
            j = (k - 7) // 2
            eacc[...] += jnp.dot(rwt[j], cg[j].reshape(256, 256), preferred_element_type=F32)

        stage(4, final)
        stage(2, x_sum)
        stage(0, x_second)

        @pl.when(k == 0)
        def _():
            back(2)

        @pl.when(k == 1)
        def _():
            from_y(3)
            back(3)

        @pl.when((k >= 2) & (k < 4))
        def _():
            for q in (2 * k - 4, 2 * k - 3):
                gt[q] = g[q].reshape(256, 576).T

        @pl.when((k >= 4) & (k < 8))
        def _():
            dec_grad(k - 4)

    shift = pl.multiple_of(64 * lax.rem(d, 2), 64)
    enc_o[0] = eacc[pl.ds(shift, 576)].astype(BF)

    @pl.loop(0, 16)
    def _(n):
        b = order(lax.rem(n, 4))
        blk = ss.at[n]

        @pl.when(t < 3)
        def _():
            sent(blk, S["a_n1"].at[n])

        @pl.when(second(b))
        def _():
            sent(blk, S["a_n2"].at[n])

        @pl.when(relays(b))
        def _():
            sent(blk, S["a_rl"].at[n])

        @pl.when(d != b)
        def _():
            sent(blk, S["zc_s"].at[n])

    @pl.loop(0, 12)
    def _(n):
        sent(ss.at[0], S["az"].at[n])
        sent(ss.at[0], S["e_s"].at[n])
        sent(own, S["yb_s"].at[n])
        sent(own, S["cy_s"].at[n])

    @pl.loop(0, 8)
    def _(u):
        @pl.when((t > 0) | (lax.rem(u, 2) == 0))
        def _():
            sent(xr.at[u], S["x_s"].at[u])

        @pl.when(t >= 2)
        def _():
            sent(xr.at[u], S["x_s"].at[8 + u])

        @pl.when(t == 3)
        def _():
            sent(xr.at[u], S["x_s"].at[16 + u])

    @pl.loop(0, 4)
    def _(j):
        sent(po.at[j], S["pc_s"].at[j])
        sent(po.at[j], S["cc_s"].at[j])

    for k in range(3):
        sent(own, S["zb_s"].at[k])
        sent(own, S["cz_s"].at[k])
        col_moves[k].wait_send()
        core_moves[k].wait_send()
    col_moves[3].wait_send()


def shards(residual, enc_weight, enc_bias, dec_weight, dec_bias, target):
    wt = jnp.swapaxes(dec_weight[:, 0], 1, 2)
    vmem = pl.BlockSpec(memory_space=pltpu.VMEM)
    hbm = pl.BlockSpec(memory_space=pl.ANY)
    enc, dec = pl.pallas_call(
        body,
        out_shape=(
            jax.ShapeDtypeStruct((1, 576, 256), BF),
            jax.ShapeDtypeStruct((4, 576, 256), BF),
        ),
        in_specs=[hbm, hbm, vmem, hbm, vmem, vmem],
        out_specs=(vmem, vmem),
        scratch_shapes=[pltpu.VMEM(*spec) for spec in SCRATCH.values()]
        + [pltpu.SemaphoreType.DMA((n,)) for n in SEMS.values()],
        compiler_params=pltpu.CompilerParams(
            collective_id=0, has_side_effects=True, vmem_limit_bytes=56 * 1024 * 1024
        ),
    )(residual, enc_weight, enc_bias, wt, dec_bias, target)
    return enc, jnp.swapaxes(dec, 1, 2)[:, None]


def solution(mesh):
    in_specs = (
        P("layer", "dp", None),
        P("layer", None, "feat"),
        P("layer", "feat"),
        P(None, "layer", "feat", "dp"),
        P("layer", "dp"),
        P("layer", "feat", "dp"),
    )
    out_specs = (P("layer", "dp", "feat"), P(None, "layer", "feat", "dp"))
    return jax.shard_map(shards, mesh=mesh, in_specs=in_specs, out_specs=out_specs, check_vma=False)
```

time: 123 us -> 114 us (0.927)
  the two profiles are of different devices: /device:TPU:6 before, /device:TPU:24 now
where the time goes in v3:
time: 114 us; the launch traced here: 113 us
  Pallas kernels  109 us (96%)
  local copies, waits for them, and re-layouts  4.05 us (4%)
    pallas_call x1, Pallas kernels, shards(): pl.pallas_call(body, out_shape=(jax.ShapeDtypeStruct((1, 576, 256), BF),...  109 us
    unnamed x2, local copies, waits for them, and re-layouts  4.05 us

profile of v3, /device:TPU:24, one launch (start us, length us, event | category | flops | bytes accessed | tf_op | source)
XLA Modules:
  0.0 113.4 jit_solution(178688972280095190)
XLA Ops:
  0.6 108.7 %shard_map.77 = (bf16[1,576,256]{2,1,0:T(8,128)(2,1)}, bf16[4,576,256]{2,1,0:T(8,128)(2,1)}) custom-call(bf16[1,256,2304]{2,1,0:T(8,128)(2,1)} %refs_0_.1, bf16[1,2304,256]{2,1,0:T(8,128)(2,1)} %refs_1_.1, f32[1,256]{1,0:T(1,128)} %refs_2_.1, bf16[4,576,256]{2,1,0:T(8,128)(2,1)} %bitcast.9, f32[1,576]{1,0:T(1,128)} %refs_4_.1, bf16[1,32,576]{2,1,0:T(8,128)(2,1)} %refs_5_.1), custom_call_target="tpu_custom_call" | custom-call | tf_op jit(solution)/shard_map/pallas_call | solution.py:548
  109.4 1.7 %copy.11 = bf16[1,576,256]{2,1,0:T(8,128)(2,1)} copy(bf16[1,576,256]{2,1,0:T(8,128)(2,1)} %get-tuple-element.10) | data formatting | bytes 589824
  111.1 2.4 %copy.12 = bf16[4,1,256,576]{2,3,1,0:T(8,128)(2,1)} copy(bf16[4,1,256,576]{2,3,1,0:T(8,128)(2,1)} %bitcast.8) | data formatting | bytes 2359296

commit v4 on v3

--- a/solution.py
+++ b/solution.py
@@ -223,19 +223,11 @@
 
     for i in range(4):
         to_line(i)
-    for i in range(2):
+    for i in range(4):
         to_layers(i, d)
 
     @pl.loop(0, 8)
     def _(k):
-        @pl.when((k >= 4) & (k < 8))
-        def _():
-            z_part(k - 4)
-
-        @pl.when((k >= 3) & (k < 7))
-        def _():
-            y_part(k - 3)
-
         @pl.when(k < 4)
         def _():
             for h in range(1, 4):
@@ -246,10 +238,6 @@
                         arrived(codes.at[t, chunk_z(k), p], S["ar"].at[t * 16 + k * 4 + p])
                         to_layers(k, b)
 
-        @pl.when(k < 2)
-        def _():
-            to_layers(k + 2, d)
-
         @pl.when((k >= 1) & (k < 5))
         def _():
             relay(k - 1, d)
@@ -259,24 +247,17 @@
                     def _():
                         relay(k - 1, b)
 
+        @pl.when((k >= 4) & (k < 8))
+        def _():
+            z_part(k - 4)
+
+        @pl.when((k >= 3) & (k < 7))
+        def _():
+            y_part(k - 3)
+
         @pl.when((k >= 2) & (k < 6))
         def _():
             recon_chunk(k - 2)
-
-        @pl.when(k == 3)
-        def _():
-            for one in col_moves:
-                one.start()
-            rw[pd] = resid[:, pl.ds(start_col(d), WIN)]
-
-        @pl.when(k == 6)
-        def _():
-            arrived(rw.at[slots[0], half], S["rr"].at[0])
-            arrived(rw.at[slots[1], half], S["rr"].at[1])
-            arrived(rw.at[slots[2], pl.ds(pl.multiple_of(c * 128, 64), 64)], S["rr"].at[2])
-            arrived(rw.at[slots[2], pl.ds(pl.multiple_of(c * 128 + 64, 64), 64)], S["rr"].at[3])
-            for one in core_moves:
-                one.start()
 
     scale = 1.0 / math.sqrt(1024)
     g = R["g"]
@@ -430,58 +411,76 @@
     for k, dev in enumerate((dev_zp, dev_zm, dev_z2)):
         copy(own, own, S["cz_s"].at[k], S["cz"].at[k], dev).start()
     to_y(0)
-    for n, k in enumerate(slots):
-        arrived(rw.at[k, other_half], S["rc"].at[n])
-
-    @pl.loop(0, 4)
-    def _(j):
-        rwt[j] = rw[:, pl.ds(pl.multiple_of(64 * block_z(j), 64), 64)].reshape(256, WIN).T
-
     eacc[...] = jnp.zeros_like(eacc)
     from_y(0)
     from_z(1)
     from_z(2)
     back(0)
-    from_z(3)
     from_y(1)
+    back(1)
     from_y(2)
-    back(1)
-
-    @pl.loop(0, 14)
+
+    @pl.loop(0, 7)
     def _(k):
         def stage(lag, step):
-            @pl.when((k >= lag) & (k < lag + 8))
-            def _():
-                step(k - lag)
-
-        stage(6, gather)
-
-        @pl.when((k >= 7) & (lax.rem(k, 2) == 1))
-        def _():
-            j = (k - 7) // 2
-            eacc[...] += jnp.dot(rwt[j], cg[j].reshape(256, 256), preferred_element_type=F32)
-
-        stage(4, final)
-        stage(2, x_sum)
+            @pl.when((k >= lag) & (k < lag + 4))
+            def _():
+                j = k - lag
+                step(2 * j)
+                step(2 * j + 1)
+
         stage(0, x_second)
 
         @pl.when(k == 0)
         def _():
             back(2)
+            from_z(3)
+            for one in col_moves:
+                one.start()
+            rw[pd] = resid[:, pl.ds(start_col(d), WIN)]
 
         @pl.when(k == 1)
         def _():
             from_y(3)
             back(3)
 
-        @pl.when((k >= 2) & (k < 4))
-        def _():
-            for q in (2 * k - 4, 2 * k - 3):
+        @pl.when(k == 2)
+        def _():
+            for q in range(4):
                 gt[q] = g[q].reshape(256, 576).T
 
-        @pl.when((k >= 4) & (k < 8))
-        def _():
-            dec_grad(k - 4)
+        @pl.when((k >= 3) & (k < 5))
+        def _():
+            dec_grad(2 * k - 6)
+            dec_grad(2 * k - 5)
+
+        stage(1, x_sum)
+
+        @pl.when(k == 2)
+        def _():
+            arrived(rw.at[slots[0], half], S["rr"].at[0])
+            arrived(rw.at[slots[1], half], S["rr"].at[1])
+            arrived(rw.at[slots[2], pl.ds(pl.multiple_of(c * 128, 64), 64)], S["rr"].at[2])
+            arrived(rw.at[slots[2], pl.ds(pl.multiple_of(c * 128 + 64, 64), 64)], S["rr"].at[3])
+            for one in core_moves:
+                one.start()
+
+        stage(2, final)
+
+        @pl.when(k == 3)
+        def _():
+            for n, m in enumerate(slots):
+                arrived(rw.at[m, other_half], S["rc"].at[n])
+
+            @pl.loop(0, 4)
+            def _(j):
+                rwt[j] = rw[:, pl.ds(pl.multiple_of(64 * block_z(j), 64), 64)].reshape(256, WIN).T
+
+        stage(3, gather)
+
+        @pl.when(k >= 3)
+        def _():
+            eacc[...] += jnp.dot(rwt[k - 3], cg[k - 3].reshape(256, 256), preferred_element_type=F32)
 
     shift = pl.multiple_of(64 * lax.rem(d, 2), 64)
     enc_o[0] = eacc[pl.ds(shift, 576)].astype(BF)
@@ -539,6 +538,14 @@
         col_moves[k].wait_send()
         core_moves[k].wait_send()
     col_moves[3].wait_send()
+
+
+def copy_out(enc, dec, enc_o, dec_o, sems):
+    moves = [pltpu.make_async_copy(enc, enc_o, sems.at[0]), pltpu.make_async_copy(dec, dec_o, sems.at[1])]
+    for one in moves:
+        one.start()
+    for one in moves:
+        one.wait()
 
 
 def shards(residual, enc_weight, enc_bias, dec_weight, dec_bias, target):
@@ -559,6 +566,13 @@
             collective_id=0, has_side_effects=True, vmem_limit_bytes=56 * 1024 * 1024
         ),
     )(residual, enc_weight, enc_bias, wt, dec_bias, target)
+    enc, dec = pl.pallas_call(
+        copy_out,
+        out_shape=(jax.ShapeDtypeStruct(enc.shape, BF), jax.ShapeDtypeStruct(dec.shape, BF)),
+        in_specs=[vmem, vmem],
+        out_specs=(hbm, hbm),
+        scratch_shapes=[pltpu.SemaphoreType.DMA((2,))],
+    )(enc, dec)
     return enc, jnp.swapaxes(dec, 1, 2)[:, None]
 
 

time: 114 us -> 108 us (0.947)
  the two profiles are of different devices: /device:TPU:24 before, /device:TPU:6 now
where the time goes in v4:
time: 108 us
  Pallas kernels  107 us (99%)
    pallas_call x1, Pallas kernels, shards(): pl.pallas_call(body, out_shape=(jax.ShapeDtypeStruct((1, 576, 256), BF),...  105 us
    pallas_call x1, Pallas kernels, shards(): pl.pallas_call(copy_out, out_shape=(jax.ShapeDtypeStruct(enc.shape, BF),...  2.5 us

profile of v4, /device:TPU:6, one launch (start us, length us, event | category | flops | bytes accessed | tf_op | source)
XLA Modules:
  0.0 107.8 jit_solution(7685359200918461551)
XLA Ops:
  0.6 104.7 %shard_map.77 = (bf16[1,576,256]{2,1,0:T(8,128)(2,1)}, bf16[4,576,256]{2,1,0:T(8,128)(2,1)}) custom-call(bf16[1,256,2304]{2,1,0:T(8,128)(2,1)} %refs_0_.1, bf16[1,2304,256]{2,1,0:T(8,128)(2,1)} %refs_1_.1, f32[1,256]{1,0:T(1,128)} %refs_2_.1, bf16[4,576,256]{2,1,0:T(8,128)(2,1)} %bitcast.8, f32[1,576]{1,0:T(1,128)} %refs_4_.1, bf16[1,32,576]{2,1,0:T(8,128)(2,1)} %refs_5_.1), custom_call_target="tpu_custom_call" | custom-call | tf_op jit(solution)/shard_map/pallas_call | solution.py:555
  105.3 2.5 %shard_map.78 = (bf16[1,576,256]{2,1,0:T(8,128)(2,1)}, bf16[4,576,256]{2,1,0:T(8,128)(2,1)}) custom-call(bf16[1,576,256]{2,1,0:T(8,128)(2,1)} %get-tuple-element.6.enc, bf16[4,576,256]{2,1,0:T(8,128)(2,1)} %get-tuple-element.7.dec), custom_call_target="tpu_custom_call" | custom-call | tf_op jit(solution)/shard_map/pallas_call | solution.py:569

commit v5 on v4

--- a/solution.py
+++ b/solution.py
@@ -449,12 +449,12 @@
             for q in range(4):
                 gt[q] = g[q].reshape(256, 576).T
 
+        stage(1, x_sum)
+
         @pl.when((k >= 3) & (k < 5))
         def _():
             dec_grad(2 * k - 6)
             dec_grad(2 * k - 5)
-
-        stage(1, x_sum)
 
         @pl.when(k == 2)
         def _():

time: 108 us -> 108 us (level)
  no operation moved by 1% of the time
where the time goes in v5:
time: 108 us
  Pallas kernels  107 us (99%)
    pallas_call x1, Pallas kernels, shards(): pl.pallas_call(body, out_shape=(jax.ShapeDtypeStruct((1, 576, 256), BF),...  105 us
    pallas_call x1, Pallas kernels, shards(): pl.pallas_call(copy_out, out_shape=(jax.ShapeDtypeStruct(enc.shape, BF),...  2.5 us

profile of v5, /device:TPU:6, one launch (start us, length us, event | category | flops | bytes accessed | tf_op | source)
XLA Modules:
  0.0 107.8 jit_solution(3886742504370077017)
XLA Ops:
  0.6 104.7 %shard_map.77 = (bf16[1,576,256]{2,1,0:T(8,128)(2,1)}, bf16[4,576,256]{2,1,0:T(8,128)(2,1)}) custom-call(bf16[1,256,2304]{2,1,0:T(8,128)(2,1)} %refs_0_.1, bf16[1,2304,256]{2,1,0:T(8,128)(2,1)} %refs_1_.1, f32[1,256]{1,0:T(1,128)} %refs_2_.1, bf16[4,576,256]{2,1,0:T(8,128)(2,1)} %bitcast.8, f32[1,576]{1,0:T(1,128)} %refs_4_.1, bf16[1,32,576]{2,1,0:T(8,128)(2,1)} %refs_5_.1), custom_call_target="tpu_custom_call" | custom-call | tf_op jit(solution)/shard_map/pallas_call | solution.py:555
  105.3 2.5 %shard_map.78 = (bf16[1,576,256]{2,1,0:T(8,128)(2,1)}, bf16[4,576,256]{2,1,0:T(8,128)(2,1)}) custom-call(bf16[1,576,256]{2,1,0:T(8,128)(2,1)} %get-tuple-element.6.enc, bf16[4,576,256]{2,1,0:T(8,128)(2,1)} %get-tuple-element.7.dec), custom_call_target="tpu_custom_call" | custom-call | tf_op jit(solution)/shard_map/pallas_call | solution.py:569

commit v6 on v5

--- a/solution.py
+++ b/solution.py
@@ -102,7 +102,6 @@
     positive = jnp.maximum(pre, 0.0)
     pos[...] = positive.reshape(4, 64, 256)
     codes[t, :, pd] = (positive * positive).astype(BF).reshape(4, 64, 256)
-    loads[2].wait()
 
     def chunk_z(i):
         return lax.rem(z + jnp.where(i == 0, 2, jnp.where(i == 1, 1, jnp.where(i == 2, 3, 0))), 4)
@@ -222,9 +221,9 @@
                 copy(zst.at[k], zb.at[k], S["zb_s"].at[k], S["zb"].at[k], dev).start()
 
     for i in range(4):
+        to_layers(i, d)
         to_line(i)
-    for i in range(4):
-        to_layers(i, d)
+    loads[2].wait()
 
     @pl.loop(0, 8)
     def _(k):

time: 108 us -> 109 us (level)
  no operation moved by 1% of the time
where the time goes in v6:
time: 109 us
  Pallas kernels  108 us (99%)
    pallas_call x1, Pallas kernels, shards(): pl.pallas_call(body, out_shape=(jax.ShapeDtypeStruct((1, 576, 256), BF),...  106 us
    pallas_call x1, Pallas kernels, shards(): pl.pallas_call(copy_out, out_shape=(jax.ShapeDtypeStruct(enc.shape, BF),...  2.5 us

profile of v6, /device:TPU:6, one launch (start us, length us, event | category | flops | bytes accessed | tf_op | source)
XLA Modules:
  0.0 108.7 jit_solution(11043099573964749461)
XLA Ops:
  0.6 105.6 %shard_map.77 = (bf16[1,576,256]{2,1,0:T(8,128)(2,1)}, bf16[4,576,256]{2,1,0:T(8,128)(2,1)}) custom-call(bf16[1,256,2304]{2,1,0:T(8,128)(2,1)} %refs_0_.1, bf16[1,2304,256]{2,1,0:T(8,128)(2,1)} %refs_1_.1, f32[1,256]{1,0:T(1,128)} %refs_2_.1, bf16[4,576,256]{2,1,0:T(8,128)(2,1)} %bitcast.8, f32[1,576]{1,0:T(1,128)} %refs_4_.1, bf16[1,32,576]{2,1,0:T(8,128)(2,1)} %refs_5_.1), custom_call_target="tpu_custom_call" | custom-call | tf_op jit(solution)/shard_map/pallas_call | solution.py:554
  106.2 2.5 %shard_map.78 = (bf16[1,576,256]{2,1,0:T(8,128)(2,1)}, bf16[4,576,256]{2,1,0:T(8,128)(2,1)}) custom-call(bf16[1,576,256]{2,1,0:T(8,128)(2,1)} %get-tuple-element.6.enc, bf16[4,576,256]{2,1,0:T(8,128)(2,1)} %get-tuple-element.7.dec), custom_call_target="tpu_custom_call" | custom-call | tf_op jit(solution)/shard_map/pallas_call | solution.py:568
